TPU v7x, 256 devices: a whole 4x4x8 slice. The times are simulated.
256 devices in a mesh: layer: 8 (over z_hi, core), fsdp: 32 (over x, z_lo, y).
Axes of the slice: x: 4, y: 4, z: 8 (z_hi: 4, z_lo: 2; z = z_hi * 2 + z_lo), core: 2. Of those that a mesh axis runs over, the one named last changes fastest.
Arguments:
- grads: bfloat16 [16, 2048, 2048], P('layer', 'fsdp'), may hold values from -6 to 6
- left_basis: bfloat16 [16, 2048, 2048], P('layer', 'fsdp'), may hold values from -6 to 6
- right_basis: bfloat16 [16, 2048, 2048], P('layer', 'fsdp'), may hold values from -6 to 6
- left_stat: bfloat16 [16, 2048, 2048], P('layer', 'fsdp'), may hold values from -6 to 6
- right_stat: bfloat16 [16, 2048, 2048], P('layer', 'fsdp'), may hold values from -6 to 6
- first_moment: float32 [16, 2048, 2048], P('layer', None, 'fsdp'), may hold values from -3 to 3
- second_moment: float32 [16, 2048, 2048], P('layer', None, 'fsdp'), may hold values from 0.05 to 1
- refresh_flags: int32 [16, 2, 2048], P('layer'), may hold values 0 or 1
Outputs:
- update: bfloat16 [16, 2048, 2048], P('layer', 'fsdp')
- new_first: float32 [16, 2048, 2048], P('layer', None, 'fsdp')
- new_second: float32 [16, 2048, 2048], P('layer', None, 'fsdp')
- new_left: bfloat16 [16, 2048, 2048], P('layer', 'fsdp')
- new_right: bfloat16 [16, 2048, 2048], P('layer', 'fsdp')
All inputs are finite; a program needn't handle non-finite values. No bound on the sum of `refresh_flags` on one device may be relied on, other than what follows from the above.
Results may differ from a plain program's by a relative error of at most 0.008.
Values may be sent and summed in bfloat16 or wider, within the bound.
No kernel may reach another device: no remote copies, remote signals or barrier semaphores. Data moves between devices by JAX's collectives and lax.ppermute only.
A program may use at most 128 MiB of HBM per device.

v0:
```python
import math

import jax
import jax.numpy as jnp
from jax import lax
from jax.experimental import pallas as pl
from jax.experimental.pallas import tpu as pltpu
from jax.sharding import Mesh, PartitionSpec as P

BF = jnp.bfloat16
F32 = jnp.float32
W = 2048
C = 64
R = 128
X = 512
ROOT = 1.0 / math.sqrt(W)
VMEM = 56 * 1024 * 1024
HBM = pl.BlockSpec(memory_space=pltpu.HBM)
INV = pl.BlockSpec(memory_space=pltpu.VMEM)
INS = pl.BlockSpec(memory_space=pltpu.SMEM)


def buffer_list():
    out = []
    for v, blocks in ((0, ((0, 0), (0, 1), (-1, 0), (1, 0), (-1, 1), (1, 1), (2, 0), (2, 1))), (1, ((0, 0), (0, 1)))):
        for dx, dz in blocks:
            out.append(([(0, dx, dz, v)], [(C, dx, dz, v)]))
    for dz in range(2):
        out.append(([(0, -1, dz, 1), (2 * C, 1, dz, 1), (4 * C, 2, dz, 1)], [(C, -1, dz, 1), (3 * C, 1, dz, 1), (5 * C, 2, dz, 1)]))
    return out


BUFFERS = buffer_list()
RIGHT, LEFT = 0, 1


def start_loads(pos, side, refs, dst, sems):
    c, x, zl = pos[0], pos[1], pos[2]
    places = offsets(pos)
    groups = []
    n = 0
    for step in (0, -1, 1, 2):
        xoff = pl.multiple_of(jnp.bitwise_and(x + step + 4, 3) * X, X)
        copies = []
        for dc in range(2):
            for buf, parts in enumerate(BUFFERS):
                for row, dx, dz, which in parts[side]:
                    if dx != step:
                        continue
                    z = jnp.bitwise_and(zl + dz, 1)
                    cc = jnp.bitwise_and(c + dc, 1)
                    off = pl.multiple_of(xoff + z * (2 * R) + cc * R + places[which], C)
                    cp = pltpu.make_async_copy(
                        refs[dc * len(BUFFERS) + buf].at[pl.ds(row, C), :],
                        dst.at[pl.ds(off, C), :],
                        sems.at[n],
                    )
                    cp.start()
                    copies.append(cp)
                    n += 1
        groups.append((xoff, copies))
    return groups


def offsets(pos):
    odd = jnp.bitwise_and(pos[3], 1)
    return pl.multiple_of(odd * C, C), pl.multiple_of((1 - odd) * C, C)


def load_rows(pos, refs, parts, dst, sems, first=32):
    copies = []
    for k, off in enumerate(offsets(pos)):
        for part, row in parts:
            cp = pltpu.make_async_copy(
                refs[k].at[pl.ds(part * C, C), :],
                dst.at[pl.ds(pl.multiple_of(row + off, C), C), :],
                sems.at[first + len(copies)],
            )
            cp.start()
            copies.append(cp)
    return copies


def multiply(groups, lhs, basis, acc):
    for i, (xoff, copies) in enumerate(groups):
        for cp in copies:
            cp.wait()

        part = jnp.dot(lhs[:, pl.ds(xoff, X)], basis[pl.ds(xoff, X), :], preferred_element_type=F32)
        if i == 0:
            acc[...] = part
        else:
            acc[...] += part


def pack_sums(power, norm, out):
    sums = jnp.sum(power * power, axis=0, keepdims=True)
    for i in range(16):
        norm[i : i + 1, :] = sums[:, i * 128 : i * 128 + 128]
    nb = norm[...].astype(BF)
    for i in range(16):
        out[i, R:, :] = nb


def refresh(blocks, power, norm, outs):
    sums = blocks[0, R:, :].astype(F32)
    for i in range(1, 16):
        sums = sums + blocks[i, R:, :].astype(F32)
    norm[...] = 1.0 / jnp.sqrt(sums / W + 1e-06)
    for i in range(16):
        cols = slice(i * R, (i + 1) * R)
        for k, out in enumerate(outs):
            out[C:R, cols] = (power[k * C : (k + 1) * C, cols] * norm[i : i + 1, :]).astype(BF)


def store_rows(pos, src, row, refs, sems, first):
    copies = []
    for k, off in enumerate(offsets(pos)):
        cp = pltpu.make_async_copy(src.at[pl.ds(pl.multiple_of(row + off, C), C), :], refs[k], sems.at[first + k])
        cp.start()
        copies.append(cp)
    return copies


def half_kernel(*args):
    pos, gs = args[0], args[1:3]
    out, power, basis, lhs, acc, norm, sems = args[-7:]
    rows = load_rows(pos, gs, ((0, 0), (1, R)), lhs, sems)
    groups = start_loads(pos, RIGHT, args[3:-7], basis, sems)
    for cp in rows:
        cp.wait()
    multiply(groups, lhs, basis, acc)
    stores = store_rows(pos, acc, R, (power.at[:C], power.at[C:]), sems, 40)
    for i in range(16):
        out[i, :R, :] = (acc[:R, i * R : (i + 1) * R] * ROOT).astype(BF)
    pack_sums(acc[R:, :], norm, out)
    for cp in stores:
        cp.wait()


def left_kernel(*args):
    pos, hcols = args[:2]
    gs, power_r = args[2:4], args[4]
    out, home0, home1, power, basis, lhs, acc, mom, dire, norm, right, sems = args[-12:]
    rows = load_rows(pos, gs, ((2, R),), lhs, sems)
    groups = start_loads(pos, LEFT, args[5:-12], basis, sems)
    later = load_rows(pos, gs, ((3, 0), (4, R)), mom, sems, 34)
    later.append(pltpu.make_async_copy(power_r, right, sems.at[42]))
    later[-1].start()
    for i in range(16):
        lhs[:R, i * R : (i + 1) * R] = hcols[i, :R, :].astype(F32).T.astype(BF)
    for cp in rows:
        cp.wait()
    multiply(groups, lhs, basis, acc)
    stores = store_rows(pos, acc, R, (power.at[:C], power.at[C:]), sems, 40)
    for cp in later:
        cp.wait()
    for i in range(16):
        cols = slice(i * R, (i + 1) * R)
        rot = acc[:R, cols] * ROOT
        nf = 0.9 * mom[:R, cols].astype(F32) + 0.1 * rot
        ns = 0.95 * mom[R:, cols].astype(F32) + 0.05 * rot * rot
        dire[cols, :] = (nf / (jnp.sqrt(ns) + 1e-8)).T.astype(BF)

    o0, o1 = offsets(pos)
    home0[:C, :] = (acc[pl.ds(o0, C), :] * ROOT).astype(BF)
    home1[:C, :] = (acc[pl.ds(o1, C), :] * ROOT).astype(BF)
    refresh(hcols, right, norm, (home0, home1))
    pack_sums(acc[R:, :], norm, out)

    @pl.loop(0, 2)
    def _(n):
        ro = pl.multiple_of(n * 1024, 1024)
        bk = (jnp.dot(basis[pl.ds(ro, 1024), :], dire[...], preferred_element_type=F32) * ROOT).astype(BF)
        for i in range(8):
            out[8 * n + i, :R, :] = bk[i * R : (i + 1) * R]

    for cp in stores:
        cp.wait()


def raw_kernel(*args):
    pos, brows, power_l = args[:3]
    home0, home1, total, basis, lhs, raw, left, norm, sems = args[-9:]
    groups = start_loads(pos, RIGHT, args[3:-9], basis, sems)
    power = pltpu.make_async_copy(power_l, left, sems.at[42])
    power.start()
    for i in range(16):
        lhs[:, i * R : (i + 1) * R] = brows[i, :R, :]
    tot = jnp.zeros((1, X), F32)
    for xoff, copies in groups:
        for cp in copies:
            cp.wait()
        r = lax.dot_general(
            lhs[...], basis[pl.ds(xoff, X), :], (((1,), (1,)), ((), ())), preferred_element_type=F32
        ) * ROOT
        tot = tot + jnp.sum(r * r, axis=0, keepdims=True)
        raw[:, pl.ds(xoff, X)] = r.astype(BF)
    o0, o1 = offsets(pos)
    home0[:C, :] = raw[pl.ds(o0, C), :]
    home1[:C, :] = raw[pl.ds(o1, C), :]
    power.wait()
    refresh(brows, left, norm, (home0, home1))
    total[...] = jnp.broadcast_to(jnp.sum(tot, axis=1, keepdims=True), (256, 128))


def sds(shape, dtype):
    return jax.ShapeDtypeStruct(shape, dtype)


def call(kernel, name, outs, in_hbm, scratch, flops, vmem_args, any_args):
    return pl.pallas_call(
        kernel,
        out_shape=outs,
        in_specs=[INS] + [INV] * (len(vmem_args) - 1) + [HBM] * len(any_args),
        out_specs=(INV,) * (len(outs) - in_hbm) + (HBM,) * in_hbm,
        scratch_shapes=scratch,
        compiler_params=pltpu.CompilerParams(vmem_limit_bytes=VMEM),
        cost_estimate=pl.CostEstimate(flops=flops, bytes_accessed=3 * W * W, transcendentals=0),
        name=name,
    )(*vmem_args, *any_args)


BASIS = pltpu.VMEM((W, W), BF)
SEMS = pltpu.SemaphoreType.DMA((43,))
NORM = pltpu.VMEM((16, 128), F32)
POWER = pltpu.VMEM((R, W), F32)
WIDE = pltpu.VMEM((2 * R, W), BF)
HOME = sds((R, W), BF)
BLOCKS = sds((16, R + 16, R), BF)


def call_half(pos, gs, pieces):
    scratch = [BASIS, WIDE, pltpu.VMEM((2 * R, W), F32), NORM, SEMS]
    outs = (BLOCKS, sds((R, W), F32))
    return call(half_kernel, "half", outs, 1, scratch, 4 * R * W * W, (pos,), (*gs, *pieces))


def call_left(pos, gs, hcols, power_r, pieces):
    scratch = [BASIS, WIDE, pltpu.VMEM((2 * R, W), F32), WIDE, pltpu.VMEM((W, R), BF), NORM, POWER, SEMS]
    outs = (BLOCKS, HOME, HOME, sds((R, W), F32))
    hbm_args = (*gs, power_r, *pieces)
    return call(left_kernel, "left", outs, 1, scratch, 6 * R * W * W, (pos, hcols), hbm_args)


def call_raw(pos, brows, power_l, pieces):
    scratch = [BASIS, pltpu.VMEM((R, W), BF), pltpu.VMEM((R, W), BF), POWER, NORM, SEMS]
    outs = (HOME, HOME, sds((256, 128), F32))
    return call(raw_kernel, "raw", outs, 0, scratch, 2 * R * W * W, (pos, brows), (power_l, *pieces))


def shift(v, by):
    return lax.ppermute(v, "x", [(i, (i + by) % 4) for i in range(4)])


def neighbours(block):
    return [shift(block, 1), shift(block, -1)]


def swap(v, axis):
    return lax.ppermute(v, axis, [(0, 1), (1, 0)])


def other_core(*blocks):
    return [swap(v, "c") for v in blocks]


def route(k):
    return [(c * 4 + 2 * h + b, h * 4 + 2 * c + (k ^ b)) for c in range(2) for h in range(2) for b in range(2)]


def there(v, k):
    return lax.ppermute(v, ("c", "y"), route(k))


def home(v, k):
    return lax.ppermute(v, ("c", "y"), [(b, a) for a, b in route(k)])


def after(v, *others):
    return lax.optimization_barrier((v,) + others)[0]


def body(grads, left_basis, right_basis, left_stat, right_stat, first_moment, second_moment, refresh_flags):
    c, x, zl, y = (lax.axis_index(a) for a in ("c", "x", "zl", "y"))
    pos = jnp.stack([c, x, zl, y]).astype(jnp.int32)
    odd = jnp.bitwise_and(y, 1)
    even = odd == 0

    def pick(a, k):
        return lax.dynamic_index_in_dim(a, jnp.bitwise_xor(odd, k), 0, keepdims=False)

    def send(*arrays):
        return [there(jnp.concatenate([pick(a, k) for a in arrays], axis=0), k) for k in range(2)]

    def collect(v0, v1):
        return jnp.where(even, jnp.stack([v0, v1]), jnp.stack([v1, v0]))

    firsts, seconds = (jnp.swapaxes(m, 1, 2) for m in (first_moment, second_moment))
    u, v = send(right_basis, left_basis)
    rest = send(after(grads, u, v), right_stat, left_stat, firsts.astype(BF), seconds.astype(BF))

    v_near = neighbours(v)
    uz = swap(u, "zl")
    u_near = neighbours(u)
    vz = swap(v, "zl")
    v_far = [shift(after(v_near[0][:C], uz), 1), shift(after(v_near[1][C:], uz), -1)]
    uz_near = neighbours(uz)
    v_all = jnp.concatenate([after(v_near[0], *u_near, vz, *rest), v_near[1], *v_far], axis=0)
    v_all_z = swap(v_all, "zl")
    far = [shift(after(u_near[0], *uz_near), 1), shift(after(uz_near[1], u_near[0]), -1)]
    pieces = [u, uz, *u_near, *uz_near, *far, v, vz, v_all, v_all_z]
    pieces += other_core(*pieces[:-1], after(v_all_z, *far))

    group = ("x", "zl", "c")
    half, power_r = call_half(pos, rest, pieces)
    hcols = lax.all_to_all(half, group, split_axis=0, concat_axis=0, tiled=True)
    back, home0, home1, power_l = call_left(pos, rest, hcols, power_r, pieces)
    brows = lax.all_to_all(back, group, split_axis=0, concat_axis=0, tiled=True)
    early = collect(home(after(home0, brows), 0), home(after(home1, brows), 1))
    home0, home1, total = call_raw(pos, brows, power_l, pieces)
    totals = lax.all_to_all(total, ("zh", "c", "x", "zl", "y"), split_axis=0, concat_axis=0, tiled=True)
    late = collect(home(home0, 0), home(home1, 1))

    def refreshed(side, part, basis):
        return jnp.where(refresh_flags[:, side, None, :] == 1, part, basis)

    new_left = refreshed(0, late[:, C:], left_basis)
    rotated = early[:, :C].astype(F32)
    new_right = refreshed(1, early[:, C:], right_basis)
    new_first = jnp.swapaxes(0.9 * firsts + 0.1 * rotated, 1, 2)
    new_second = jnp.swapaxes(0.95 * seconds + 0.05 * rotated * rotated, 1, 2)

    totals = after(totals, new_left, new_right, new_first, new_second)
    count = lax.axis_size(("zh", "c")) * 2 * W * W
    rms = jnp.sqrt(jnp.sum(totals[:, 0]) / count + 1e-06)
    factor = jnp.minimum(1.0, 0.5 / rms)
    update = (late[:, :C].astype(F32) * factor).astype(BF)
    return update, new_first, new_second, new_left, new_right


def solution(mesh):
    fine = Mesh(mesh.devices.reshape(4, 2, 4, 2, 4), ("zh", "c", "x", "zl", "y"))
    layer, fsdp = ("zh", "c"), ("x", "zl", "y")
    rows, cols = P(layer, fsdp, None), P(layer, None, fsdp)
    return jax.shard_map(
        body,
        mesh=fine,
        in_specs=(rows,) * 5 + (cols,) * 2 + (P(layer, None, None),),
        out_specs=(rows, cols, cols, rows, rows),
        check_vma=False,
    )
```

profile of v0, /device:TPU:1, one launch (start us, length us, event | category | flops | bytes accessed | tf_op | source)
XLA Modules:
  0.0 192.1 jit_solution(11357527468389323449)
XLA Ops:
  2.0 4.2 %collective-permute-start.1 = (bf16[128,2048]{1,0:T(8,128)(2,1)S(1)}, bf16[128,2048]{1,0:T(8,128)(2,1)S(1)}, u32[]{:S(2)}, u32[]{:S(2)}) collective-permute-start(bf16[128,2048]{1,0:T(8,128)(2,1)S(1)} %pad_maximum_fusion.1), channel_id=1, source_target_pairs={{0,1},{1,0},{2,33},{3,32},{32,3},{33,2},{34,35},{35,34},{4,5},{5,4... | collective-permute-start | bytes 1572872 | tf_op jit(solution)/shard_map/ppermute | solution.py:273
  6.3 2.2 %collective-permute-start = (bf16[128,2048]{1,0:T(8,128)(2,1)S(1)}, bf16[128,2048]{1,0:T(8,128)(2,1)S(1)}, u32[]{:S(2)}, u32[]{:S(2)}) collective-permute-start(bf16[128,2048]{1,0:T(8,128)(2,1)S(1)} %pad_maximum_fusion), channel_id=1, source_target_pairs={{0,0},{1,1},{2,32},{3,33},{32,2},{33,3},{34,34},{35,35},{4,4},{5,5... | collective-permute-start | bytes 1572872 | tf_op jit(solution)/shard_map/ppermute | solution.py:273
  8.7 6.6 %collective-permute-done.1.args_11_.args_13_ = bf16[128,2048]{1,0:T(8,128)(2,1)S(1)} collective-permute-done((bf16[128,2048]{1,0:T(8,128)(2,1)S(1)}, bf16[128,2048]{1,0:T(8,128)(2,1)S(1)}, u32[]{:S(2)}, u32[]{:S(2)}) %collective-permute-start.1) | collective-permute-done | bytes 524320 | tf_op jit(solution)/shard_map/ppermute | solution.py:273
  15.3 4.8 %collective-permute-done.args_3_.args_5_ = bf16[128,2048]{1,0:T(8,128)(2,1)S(1)} collective-permute-done((bf16[128,2048]{1,0:T(8,128)(2,1)S(1)}, bf16[128,2048]{1,0:T(8,128)(2,1)S(1)}, u32[]{:S(2)}, u32[]{:S(2)}) %collective-permute-start) | collective-permute-done | bytes 524320 | tf_op jit(solution)/shard_map/ppermute | solution.py:273
  20.5 3.0 %collective-permute-start.2 = (bf16[320,2048]{1,0:T(8,128)(2,1)S(1)}, bf16[320,2048]{1,0:T(8,128)(2,1)S(1)}, u32[]{:S(2)}, u32[]{:S(2)}) collective-permute-start(bf16[320,2048]{1,0:T(8,128)(2,1)S(1)} %get-tuple-element.46), channel_id=1, source_target_pairs={{0,0},{1,1},{2,32},{3,33},{32,2},{33,3},{34,34},{35,35},{4,4},{5,5... | collective-permute-start | bytes 3932168 | tf_op jit(solution)/shard_map/ppermute | solution.py:273
  29.3 6.1 %collective-permute-done.12 = bf16[128,2048]{1,0:T(8,128)(2,1)S(1)} collective-permute-done((bf16[128,2048]{1,0:T(8,128)(2,1)S(1)}, bf16[128,2048]{1,0:T(8,128)(2,1)S(1)}, u32[]{:S(2)}, u32[]{:S(2)}) %collective-permute-start.12) | collective-permute-done | bytes 524320 | tf_op jit(solution)/shard_map/ppermute | solution.py:253
  36.5 2.7 %collective-permute-start.11 = (bf16[128,2048]{1,0:T(8,128)(2,1)S(1)}, bf16[128,2048]{1,0:T(8,128)(2,1)S(1)}, u32[]{:S(2)}, u32[]{:S(2)}) collective-permute-start(bf16[128,2048]{1,0:T(8,128)(2,1)S(1)} %collective-permute-done.1.args_11_.args_13_), channel_id=1, source_target_pairs={{0,4},{4,0},{1,5},{5,1},{2,6},{6,2},{3,7},{7,3},{8,12},{12,8},{9,1... | collective-permute-start | bytes 1572872 | tf_op jit(solution)/shard_map/ppermute | solution.py:261
  40.8 5.4 %collective-permute-done.5.args_5_.args_7_ = bf16[128,2048]{1,0:T(8,128)(2,1)S(1)} collective-permute-done((bf16[128,2048]{1,0:T(8,128)(2,1)S(1)}, bf16[128,2048]{1,0:T(8,128)(2,1)S(1)}, u32[]{:S(2)}, u32[]{:S(2)}) %collective-permute-start.5) | collective-permute-done | bytes 524320 | tf_op jit(solution)/shard_map/ppermute | solution.py:253
  50.4 5.1 %collective-permute-done.3.args_2_.args_3_ = bf16[320,2048]{1,0:T(8,128)(2,1)} collective-permute-done((bf16[320,2048]{1,0:T(8,128)(2,1)S(1)}, bf16[320,2048]{1,0:T(8,128)(2,1)}, u32[]{:S(2)}, u32[]{:S(2)}) %collective-permute-start.3) | collective-permute-done | bytes 1310752 | tf_op jit(solution)/shard_map/ppermute | solution.py:273
  55.7 1.6 collective-permute-start.16
  57.3 2.5 %collective-permute-start.8 = (bf16[128,2048]{1,0:T(8,128)(2,1)S(1)}, bf16[128,2048]{1,0:T(8,128)(2,1)S(1)}, u32[]{:S(2)}, u32[]{:S(2)}) collective-permute-start(bf16[128,2048]{1,0:T(8,128)(2,1)S(1)} %collective-permute-done.4.args_4_.args_6_), channel_id=1, source_target_pairs={{0,24},{8,0},{16,8},{24,16},{1,25},{9,1},{17,9},{25,17},{2,26},{10... | collective-permute-start | bytes 1572872 | tf_op jit(solution)/shard_map/ppermute | solution.py:253
  59.8 8.4 %collective-permute-done.8.args_8_.args_10_ = bf16[128,2048]{1,0:T(8,128)(2,1)S(1)} collective-permute-done((bf16[128,2048]{1,0:T(8,128)(2,1)S(1)}, bf16[128,2048]{1,0:T(8,128)(2,1)S(1)}, u32[]{:S(2)}, u32[]{:S(2)}) %collective-permute-start.8) | collective-permute-done | bytes 524320 | tf_op jit(solution)/shard_map/ppermute | solution.py:253
  68.3 2.4 %collective-permute-done.7.args_7_.args_9_ = bf16[128,2048]{1,0:T(8,128)(2,1)} collective-permute-done((bf16[128,2048]{1,0:T(8,128)(2,1)S(1)}, bf16[128,2048]{1,0:T(8,128)(2,1)}, u32[]{:S(2)}, u32[]{:S(2)}) %collective-permute-start.7) | collective-permute-done | bytes 524320 | tf_op jit(solution)/shard_map/ppermute | solution.py:253
  70.7 2.7 %collective-permute-start.10 = (bf16[128,2048]{1,0:T(8,128)(2,1)S(1)}, bf16[128,2048]{1,0:T(8,128)(2,1)}, u32[]{:S(2)}, u32[]{:S(2)}) collective-permute-start(bf16[128,2048]{1,0:T(8,128)(2,1)S(1)} %collective-permute-done.8.args_8_.args_10_), channel_id=1, source_target_pairs={{0,24},{8,0},{16,8},{24,16},{1,25},{9,1},{17,9},{25,17},{2,26},{10... | collective-permute-start | bytes 1572872 | tf_op jit(solution)/shard_map/ppermute | solution.py:253
  73.9 8.7 %collective-permute-done.9.args_9_.args_11_ = bf16[128,2048]{1,0:T(8,128)(2,1)} collective-permute-done((bf16[128,2048]{1,0:T(8,128)(2,1)S(1)}, bf16[128,2048]{1,0:T(8,128)(2,1)}, u32[]{:S(2)}, u32[]{:S(2)}) %collective-permute-start.9) | collective-permute-done | bytes 524320 | tf_op jit(solution)/shard_map/ppermute | solution.py:253
  83.1 6.4 %collective-permute-done.16.args_14_.args_16_ = bf16[384,2048]{1,0:T(8,128)(2,1)S(1)} collective-permute-done((bf16[384,2048]{1,0:T(8,128)(2,1)S(1)}, bf16[384,2048]{1,0:T(8,128)(2,1)S(1)}, u32[]{:S(2)}, u32[]{:S(2)}) %collective-permute-start.16) | collective-permute-done | bytes 1572896 | tf_op jit(solution)/shard_map/ppermute | solution.py:261
  90.8 3.6 %collective-permute-done.26.args_24_.args_26_ = bf16[128,2048]{1,0:T(8,128)(2,1)S(1)} collective-permute-done((bf16[128,2048]{1,0:T(8,128)(2,1)S(1)}, bf16[128,2048]{1,0:T(8,128)(2,1)S(1)}, u32[]{:S(2)}, u32[]{:S(2)}) %collective-permute-start.26) | collective-permute-done | bytes 524320 | tf_op jit(solution)/shard_map/ppermute | solution.py:261
  96.1 2.1 %collective-permute-done.22.args_20_.args_22_ = bf16[128,2048]{1,0:T(8,128)(2,1)S(1)} collective-permute-done((bf16[128,2048]{1,0:T(8,128)(2,1)S(1)}, bf16[128,2048]{1,0:T(8,128)(2,1)S(1)}, u32[]{:S(2)}, u32[]{:S(2)}) %collective-permute-start.22) | collective-permute-done | bytes 524320 | tf_op jit(solution)/shard_map/ppermute | solution.py:261
  101.3 7.2 %half.1 = (bf16[16,144,128]{2,1,0:T(8,128)(2,1)}, f32[128,2048]{1,0:T(8,128)}) custom-call(s32[4]{0:T(128)} %pad_add_fusion.args_0_, bf16[320,2048]{1,0:T(8,128)(2,1)} %copy-done.2, bf16[320,2048]{1,0:T(8,128)(2,1)} %collective-permute-done.3.args_2_.args_3_, bf16[128,2048]{1,0:T(8,128)(2,1)} %copy-done.4, bf16[128,2048]{1,0:T(8,128)(2,1)} %copy-done.5, ...), custom_call_target="tpu_custom_call" | custom-call | flops 2147483648 | bytes 12582912 | tf_op jit(solution)/shard_map/half/pallas_call | solution.py:212
  108.5 15.5 %all_to_all.22.args_1_ = bf16[16,144,128]{2,1,0:T(8,128)(2,1)} all-to-all(bf16[16,144,128]{2,1,0:T(8,128)(2,1)} %get-tuple-element.31), channel_id=1, replica_groups=mesh['zh'=4,'c'=2,'x'=4,'zl'=2,'y'=4] {'x','zl','c'}, dimensions={0} | all-to-all | bytes 1179648 | tf_op jit(solution)/shard_map/all_to_all | solution.py:317
  124.1 10.6 %left.1 = (bf16[16,144,128]{2,1,0:T(8,128)(2,1)}, bf16[128,2048]{1,0:T(8,128)(2,1)}, bf16[128,2048]{1,0:T(8,128)(2,1)}, f32[128,2048]{1,0:T(8,128)}) custom-call(s32[4]{0:T(128)} %pad_add_fusion.args_0_, bf16[16,144,128]{2,1,0:T(8,128)(2,1)} %all_to_all.22.args_1_, bf16[320,2048]{1,0:T(8,128)(2,1)} %copy-done.2, ...), custom_call_target="tpu_custom_call" | custom-call | flops 3221225472 | bytes 12582912 | tf_op jit(solution)/shard_map/left/pallas_call | solution.py:212
  134.7 4.0 %all-to-all-start.1 = ((bf16[16,144,128]{2,1,0:T(8,128)(2,1)}), bf16[16,144,128]{2,1,0:T(8,128)(2,1)S(1)}, u32[]{:S(2)}, u32[]{:S(2)}) async-start(bf16[16,144,128]{2,1,0:T(8,128)(2,1)} %get-tuple-element.33), calls=%async_computation.1 | async-start | bytes 1179648 | tf_op jit(solution)/shard_map/all_to_all | solution.py:319
  138.8 10.6 %all-to-all-done.1.args_1_ = bf16[16,144,128]{2,1,0:T(8,128)(2,1)S(1)} async-done(((bf16[16,144,128]{2,1,0:T(8,128)(2,1)}), bf16[16,144,128]{2,1,0:T(8,128)(2,1)S(1)}, u32[]{:S(2)}, u32[]{:S(2)}) %all-to-all-start.1) | async-done | bytes 589856 | tf_op jit(solution)/shard_map/all_to_all | solution.py:319
  149.3 3.7 %collective-permute-start.31 = (bf16[128,2048]{1,0:T(8,128)(2,1)}, bf16[128,2048]{1,0:T(8,128)(2,1)S(1)}, u32[]{:S(2)}, u32[]{:S(2)}) collective-permute-start(bf16[128,2048]{1,0:T(8,128)(2,1)} %get-tuple-element.39), channel_id=1, source_target_pairs={{0,0},{1,1},{32,2},{33,3},{2,32},{3,33},{34,34},{35,35},{4,4},{5,5... | collective-permute-start | bytes 1572872 | tf_op jit(solution)/shard_map/ppermute | solution.py:277
  153.0 5.5 %collective-permute-start.32 = (bf16[128,2048]{1,0:T(8,128)(2,1)}, bf16[128,2048]{1,0:T(8,128)(2,1)S(1)}, u32[]{:S(2)}, u32[]{:S(2)}) collective-permute-start(bf16[128,2048]{1,0:T(8,128)(2,1)} %get-tuple-element.41), channel_id=1, source_target_pairs={{1,0},{0,1},{33,2},{32,3},{3,32},{2,33},{35,34},{34,35},{5,4},{4,5... | collective-permute-start | bytes 1572872 | tf_op jit(solution)/shard_map/ppermute | solution.py:277
  158.5 7.7 %raw.1 = (bf16[128,2048]{1,0:T(8,128)(2,1)}, bf16[128,2048]{1,0:T(8,128)(2,1)}, f32[256,128]{1,0:T(8,128)}) custom-call(s32[4]{0:T(128)} %pad_add_fusion.args_0_, bf16[16,144,128]{2,1,0:T(8,128)(2,1)} %copy-done.21, f32[128,2048]{1,0:T(8,128)} %get-tuple-element.34.args_2_, bf16[128,2048]{1,0:T(8,128)(2,1)} %copy-done.4, bf16[128,2048]{1,0:T(8,128)(2,1)} %copy-done.5, ...), custom_call_target="tpu_custom_call" | custom-call | flops 1073741824 | bytes 12582912 | tf_op jit(solution)/shard_map/raw/pallas_call | solution.py:212
  166.2 2.1 %collective-permute-start.29 = (bf16[128,2048]{1,0:T(8,128)(2,1)}, bf16[128,2048]{1,0:T(8,128)(2,1)}, u32[]{:S(2)}, u32[]{:S(2)}) collective-permute-start(bf16[128,2048]{1,0:T(8,128)(2,1)} %get-tuple-element.35), channel_id=1, source_target_pairs={{0,0},{1,1},{32,2},{33,3},{2,32},{3,33},{34,34},{35,35},{4,4},{5,5... | collective-permute-start | bytes 1572872 | tf_op jit(solution)/shard_map/ppermute | solution.py:277
  168.4 8.7 %all-to-all-start.2 = ((f32[256,1,128]{2,1,0:T(1,128)}), f32[256,1,128]{2,1,0:T(1,128)S(1)}, u32[]{:S(2)}, u32[]{:S(2)}) async-start(f32[256,1,128]{2,1,0:T(1,128)} %bitcast.63), calls=%async_computation.2 | async-start | bytes 262144 | tf_op jit(solution)/shard_map/all_to_all | solution.py:322
  177.3 1.6 fusion.3
  179.9 5.0 %collective-permute-done.30 = bf16[128,2048]{1,0:T(8,128)(2,1)} collective-permute-done((bf16[128,2048]{1,0:T(8,128)(2,1)}, bf16[128,2048]{1,0:T(8,128)(2,1)}, u32[]{:S(2)}, u32[]{:S(2)}) %collective-permute-start.30) | collective-permute-done | bytes 524320 | tf_op jit(solution)/shard_map/ppermute | solution.py:277
  184.8 1.7 maximum_select_fusion
  187.4 2.4 %all-to-all-done.2 = f32[256,1,128]{2,1,0:T(1,128)S(1)} async-done(((f32[256,1,128]{2,1,0:T(1,128)}), f32[256,1,128]{2,1,0:T(1,128)S(1)}, u32[]{:S(2)}, u32[]{:S(2)}) %all-to-all-start.2) | async-done | bytes 131104 | tf_op jit(solution)/shard_map/all_to_all | solution.py:322
  (124 shorter events, 25.3 us)
Async XLA Ops:
  2.0 13.3 %collective-permute-start.1 = (bf16[128,2048]{1,0:T(8,128)(2,1)S(1)}, bf16[128,2048]{1,0:T(8,128)(2,1)S(1)}, u32[]{:S(2)}, u32[]{:S(2)}) collective-permute-start(bf16[128,2048]{1,0:T(8,128)(2,1)S(1)} %pad_maximum_fusion.1), channel_id=1, source_target_pairs={{0,1},{1,0},{2,33},{3,32},{32,3},{33,2},{34,35},{35,34},{4,5},{5,4... | collective-permute-start | bytes 1572872 | tf_op jit(solution)/shard_map/ppermute | solution.py:273
  6.3 13.9 %collective-permute-start = (bf16[128,2048]{1,0:T(8,128)(2,1)S(1)}, bf16[128,2048]{1,0:T(8,128)(2,1)S(1)}, u32[]{:S(2)}, u32[]{:S(2)}) collective-permute-start(bf16[128,2048]{1,0:T(8,128)(2,1)S(1)} %pad_maximum_fusion), channel_id=1, source_target_pairs={{0,0},{1,1},{2,32},{3,33},{32,2},{33,3},{34,34},{35,35},{4,4},{5,5... | collective-permute-start | bytes 1572872 | tf_op jit(solution)/shard_map/ppermute | solution.py:273
  20.5 28.8 %collective-permute-start.2 = (bf16[320,2048]{1,0:T(8,128)(2,1)S(1)}, bf16[320,2048]{1,0:T(8,128)(2,1)S(1)}, u32[]{:S(2)}, u32[]{:S(2)}) collective-permute-start(bf16[320,2048]{1,0:T(8,128)(2,1)S(1)} %get-tuple-element.46), channel_id=1, source_target_pairs={{0,0},{1,1},{2,32},{3,33},{32,2},{33,3},{34,34},{35,35},{4,4},{5,5... | collective-permute-start | bytes 3932168 | tf_op jit(solution)/shard_map/ppermute | solution.py:273
  23.5 32.1 %collective-permute-start.3 = (bf16[320,2048]{1,0:T(8,128)(2,1)S(1)}, bf16[320,2048]{1,0:T(8,128)(2,1)}, u32[]{:S(2)}, u32[]{:S(2)}) collective-permute-start(bf16[320,2048]{1,0:T(8,128)(2,1)S(1)} %get-tuple-element.45), channel_id=1, source_target_pairs={{0,1},{1,0},{2,33},{3,32},{32,3},{33,2},{34,35},{35,34},{4,5},{5,4... | collective-permute-start | bytes 3932168 | tf_op jit(solution)/shard_map/ppermute | solution.py:273
  25.0 10.4 %collective-permute-start.12 = (bf16[128,2048]{1,0:T(8,128)(2,1)S(1)}, bf16[128,2048]{1,0:T(8,128)(2,1)S(1)}, u32[]{:S(2)}, u32[]{:S(2)}) collective-permute-start(bf16[128,2048]{1,0:T(8,128)(2,1)S(1)} %collective-permute-done.1.args_11_.args_13_), channel_id=1, source_target_pairs={{0,8},{8,16},{16,24},{24,0},{1,9},{9,17},{17,25},{25,1},{2,10},{10... | collective-permute-start | bytes 1572872 | tf_op jit(solution)/shard_map/ppermute | solution.py:253
  26.2 10.3 %collective-permute-start.13 = (bf16[128,2048]{1,0:T(8,128)(2,1)S(1)}, bf16[128,2048]{1,0:T(8,128)(2,1)S(1)}, u32[]{:S(2)}, u32[]{:S(2)}) collective-permute-start(bf16[128,2048]{1,0:T(8,128)(2,1)S(1)} %collective-permute-done.1.args_11_.args_13_), channel_id=1, source_target_pairs={{0,24},{8,0},{16,8},{24,16},{1,25},{9,1},{17,9},{25,17},{2,26},{10... | collective-permute-start | bytes 1572872 | tf_op jit(solution)/shard_map/ppermute | solution.py:253
  27.7 13.1 %collective-permute-start.4 = (bf16[128,2048]{1,0:T(8,128)(2,1)S(1)}, bf16[128,2048]{1,0:T(8,128)(2,1)S(1)}, u32[]{:S(2)}, u32[]{:S(2)}) collective-permute-start(bf16[128,2048]{1,0:T(8,128)(2,1)S(1)} %collective-permute-done.args_3_.args_5_), channel_id=1, source_target_pairs={{0,4},{4,0},{1,5},{5,1},{2,6},{6,2},{3,7},{7,3},{8,12},{12,8},{9,1... | collective-permute-start | bytes 1572872 | tf_op jit(solution)/shard_map/ppermute | solution.py:261
  35.4 10.9 %collective-permute-start.5 = (bf16[128,2048]{1,0:T(8,128)(2,1)S(1)}, bf16[128,2048]{1,0:T(8,128)(2,1)S(1)}, u32[]{:S(2)}, u32[]{:S(2)}) collective-permute-start(bf16[128,2048]{1,0:T(8,128)(2,1)S(1)} %collective-permute-done.args_3_.args_5_), channel_id=1, source_target_pairs={{0,8},{8,16},{16,24},{24,0},{1,9},{9,17},{17,25},{25,1},{2,10},{10... | collective-permute-start | bytes 1572872 | tf_op jit(solution)/shard_map/ppermute | solution.py:253
  36.5 12.0 %collective-permute-start.11 = (bf16[128,2048]{1,0:T(8,128)(2,1)S(1)}, bf16[128,2048]{1,0:T(8,128)(2,1)S(1)}, u32[]{:S(2)}, u32[]{:S(2)}) collective-permute-start(bf16[128,2048]{1,0:T(8,128)(2,1)S(1)} %collective-permute-done.1.args_11_.args_13_), channel_id=1, source_target_pairs={{0,4},{4,0},{1,5},{5,1},{2,6},{6,2},{3,7},{7,3},{8,12},{12,8},{9,1... | collective-permute-start | bytes 1572872 | tf_op jit(solution)/shard_map/ppermute | solution.py:261
  40.7 8.5 %collective-permute-start.6 = (bf16[128,2048]{1,0:T(8,128)(2,1)S(1)}, bf16[128,2048]{1,0:T(8,128)(2,1)S(1)}, u32[]{:S(2)}, u32[]{:S(2)}) collective-permute-start(bf16[128,2048]{1,0:T(8,128)(2,1)S(1)} %collective-permute-done.args_3_.args_5_), channel_id=1, source_target_pairs={{0,24},{8,0},{16,8},{24,16},{1,25},{9,1},{17,9},{25,17},{2,26},{10... | collective-permute-start | bytes 1572872 | tf_op jit(solution)/shard_map/ppermute | solution.py:253
  46.2 9.4 %collective-permute-start.14 = (bf16[64,2048]{1,0:T(8,128)(2,1)S(1)}, bf16[64,2048]{1,0:T(8,128)(2,1)S(1)}, u32[]{:S(2)}, u32[]{:S(2)}) collective-permute-start(bf16[64,2048]{1,0:T(8,128)(2,1)S(1)} %slice.36), channel_id=1, source_target_pairs={{0,8},{8,16},{16,24},{24,0},{1,9},{9,17},{17,25},{25,1},{2,10},{10... | collective-permute-start | bytes 786440 | tf_op jit(solution)/shard_map/ppermute | solution.py:253
  48.5 7.1 %collective-permute-start.15 = (bf16[64,2048]{1,0:T(8,128)(2,1)S(1)}, bf16[64,2048]{1,0:T(8,128)(2,1)S(1)}, u32[]{:S(2)}, u32[]{:S(2)}) collective-permute-start(bf16[64,2048]{1,0:T(8,128)(2,1)S(1)} %slice.37), channel_id=1, source_target_pairs={{0,24},{8,0},{16,8},{24,16},{1,25},{9,1},{17,9},{25,17},{2,26},{10... | collective-permute-start | bytes 786440 | tf_op jit(solution)/shard_map/ppermute | solution.py:253
  55.7 33.8 %collective-permute-start.16 = (bf16[384,2048]{1,0:T(8,128)(2,1)S(1)}, bf16[384,2048]{1,0:T(8,128)(2,1)S(1)}, u32[]{:S(2)}, u32[]{:S(2)}) collective-permute-start(bf16[384,2048]{1,0:T(8,128)(2,1)S(1)} %constant_dynamic-update-slice_fusion.args_13_.args_15_), channel_id=1, source_target_pairs={{0,4},{4,0},{1,5},{5,1},{2,6},{6,2},{3,7},{7,3},{8,12},{12,8},{9,1... | collective-permute-start | bytes 4718600 | tf_op jit(solution)/shard_map/ppermute | solution.py:261
  57.3 10.9 %collective-permute-start.8 = (bf16[128,2048]{1,0:T(8,128)(2,1)S(1)}, bf16[128,2048]{1,0:T(8,128)(2,1)S(1)}, u32[]{:S(2)}, u32[]{:S(2)}) collective-permute-start(bf16[128,2048]{1,0:T(8,128)(2,1)S(1)} %collective-permute-done.4.args_4_.args_6_), channel_id=1, source_target_pairs={{0,24},{8,0},{16,8},{24,16},{1,25},{9,1},{17,9},{25,17},{2,26},{10... | collective-permute-start | bytes 1572872 | tf_op jit(solution)/shard_map/ppermute | solution.py:253
  59.8 10.8 %collective-permute-start.7 = (bf16[128,2048]{1,0:T(8,128)(2,1)S(1)}, bf16[128,2048]{1,0:T(8,128)(2,1)}, u32[]{:S(2)}, u32[]{:S(2)}) collective-permute-start(bf16[128,2048]{1,0:T(8,128)(2,1)S(1)} %collective-permute-done.4.args_4_.args_6_), channel_id=1, source_target_pairs={{0,8},{8,16},{16,24},{24,0},{1,9},{9,17},{17,25},{25,1},{2,10},{10... | collective-permute-start | bytes 1572872 | tf_op jit(solution)/shard_map/ppermute | solution.py:253
  70.7 11.9 %collective-permute-start.9 = (bf16[128,2048]{1,0:T(8,128)(2,1)S(1)}, bf16[128,2048]{1,0:T(8,128)(2,1)}, u32[]{:S(2)}, u32[]{:S(2)}) collective-permute-start(bf16[128,2048]{1,0:T(8,128)(2,1)S(1)} %collective-permute-done.5.args_5_.args_7_), channel_id=1, source_target_pairs={{0,8},{8,16},{16,24},{24,0},{1,9},{9,17},{17,25},{25,1},{2,10},{10... | collective-permute-start | bytes 1572872 | tf_op jit(solution)/shard_map/ppermute | solution.py:253
  70.7 11.9 %collective-permute-start.10 = (bf16[128,2048]{1,0:T(8,128)(2,1)S(1)}, bf16[128,2048]{1,0:T(8,128)(2,1)}, u32[]{:S(2)}, u32[]{:S(2)}) collective-permute-start(bf16[128,2048]{1,0:T(8,128)(2,1)S(1)} %collective-permute-done.8.args_8_.args_10_), channel_id=1, source_target_pairs={{0,24},{8,0},{16,8},{24,16},{1,25},{9,1},{17,9},{25,17},{2,26},{10... | collective-permute-start | bytes 1572872 | tf_op jit(solution)/shard_map/ppermute | solution.py:253
  73.3 16.2 %collective-permute-start.25 = (bf16[128,2048]{1,0:T(8,128)(2,1)S(1)}, bf16[128,2048]{1,0:T(8,128)(2,1)S(1)}, u32[]{:S(2)}, u32[]{:S(2)}) collective-permute-start(bf16[128,2048]{1,0:T(8,128)(2,1)S(1)} %collective-permute-done.1.args_11_.args_13_), channel_id=1, source_target_pairs={{0,32},{32,0},{1,33},{33,1},{2,34},{34,2},{3,35},{35,3},{4,36},{36... | collective-permute-start | bytes 1572872 | tf_op jit(solution)/shard_map/ppermute | solution.py:261
  73.3 16.7 %collective-permute-start.17 = (bf16[128,2048]{1,0:T(8,128)(2,1)S(1)}, bf16[128,2048]{1,0:T(8,128)(2,1)S(1)}, u32[]{:S(2)}, u32[]{:S(2)}) collective-permute-start(bf16[128,2048]{1,0:T(8,128)(2,1)S(1)} %collective-permute-done.args_3_.args_5_), channel_id=1, source_target_pairs={{0,32},{32,0},{1,33},{33,1},{2,34},{34,2},{3,35},{35,3},{4,36},{36... | collective-permute-start | bytes 1572872 | tf_op jit(solution)/shard_map/ppermute | solution.py:261
  82.6 7.6 %collective-permute-start.18 = (bf16[128,2048]{1,0:T(8,128)(2,1)S(1)}, bf16[128,2048]{1,0:T(8,128)(2,1)S(1)}, u32[]{:S(2)}, u32[]{:S(2)}) collective-permute-start(bf16[128,2048]{1,0:T(8,128)(2,1)S(1)} %collective-permute-done.4.args_4_.args_6_), channel_id=1, source_target_pairs={{0,32},{32,0},{1,33},{33,1},{2,34},{34,2},{3,35},{35,3},{4,36},{36... | collective-permute-start | bytes 1572872 | tf_op jit(solution)/shard_map/ppermute | solution.py:261
  82.6 8.0 %collective-permute-start.19 = (bf16[128,2048]{1,0:T(8,128)(2,1)S(1)}, bf16[128,2048]{1,0:T(8,128)(2,1)S(1)}, u32[]{:S(2)}, u32[]{:S(2)}) collective-permute-start(bf16[128,2048]{1,0:T(8,128)(2,1)S(1)} %collective-permute-done.5.args_5_.args_7_), channel_id=1, source_target_pairs={{0,32},{32,0},{1,33},{33,1},{2,34},{34,2},{3,35},{35,3},{4,36},{36... | collective-permute-start | bytes 1572872 | tf_op jit(solution)/shard_map/ppermute | solution.py:261
  89.5 11.8 %collective-permute-start.27 = (bf16[384,2048]{1,0:T(8,128)(2,1)S(1)}, bf16[384,2048]{1,0:T(8,128)(2,1)}, u32[]{:S(2)}, u32[]{:S(2)}) collective-permute-start(bf16[384,2048]{1,0:T(8,128)(2,1)S(1)} %constant_dynamic-update-slice_fusion.args_13_.args_15_), channel_id=1, source_target_pairs={{0,32},{32,0},{1,33},{33,1},{2,34},{34,2},{3,35},{35,3},{4,36},{36... | collective-permute-start | bytes 4718600 | tf_op jit(solution)/shard_map/ppermute | solution.py:261
  89.5 11.7 %collective-permute-start.28 = (bf16[384,2048]{1,0:T(8,128)(2,1)S(1)}, bf16[384,2048]{1,0:T(8,128)(2,1)}, u32[]{:S(2)}, u32[]{:S(2)}) collective-permute-start(bf16[384,2048]{1,0:T(8,128)(2,1)S(1)} %collective-permute-done.16.args_14_.args_16_), channel_id=1, source_target_pairs={{0,32},{32,0},{1,33},{33,1},{2,34},{34,2},{3,35},{35,3},{4,36},{36... | collective-permute-start | bytes 4718600 | tf_op jit(solution)/shard_map/ppermute | solution.py:261
  90.2 5.8 %collective-permute-start.20 = (bf16[128,2048]{1,0:T(8,128)(2,1)S(1)}, bf16[128,2048]{1,0:T(8,128)(2,1)S(1)}, u32[]{:S(2)}, u32[]{:S(2)}) collective-permute-start(bf16[128,2048]{1,0:T(8,128)(2,1)S(1)} %collective-permute-done.6.args_6_.args_8_), channel_id=1, source_target_pairs={{0,32},{32,0},{1,33},{33,1},{2,34},{34,2},{3,35},{35,3},{4,36},{36... | collective-permute-start | bytes 1572872 | tf_op jit(solution)/shard_map/ppermute | solution.py:261
  90.6 7.5 %collective-permute-start.22 = (bf16[128,2048]{1,0:T(8,128)(2,1)S(1)}, bf16[128,2048]{1,0:T(8,128)(2,1)S(1)}, u32[]{:S(2)}, u32[]{:S(2)}) collective-permute-start(bf16[128,2048]{1,0:T(8,128)(2,1)S(1)} %collective-permute-done.8.args_8_.args_10_), channel_id=1, source_target_pairs={{0,32},{32,0},{1,33},{33,1},{2,34},{34,2},{3,35},{35,3},{4,36},{36... | collective-permute-start | bytes 1572872 | tf_op jit(solution)/shard_map/ppermute | solution.py:261
  94.4 5.4 %collective-permute-start.21 = (bf16[128,2048]{1,0:T(8,128)(2,1)}, bf16[128,2048]{1,0:T(8,128)(2,1)}, u32[]{:S(2)}, u32[]{:S(2)}) collective-permute-start(bf16[128,2048]{1,0:T(8,128)(2,1)} %collective-permute-done.7.args_7_.args_9_), channel_id=1, source_target_pairs={{0,32},{32,0},{1,33},{33,1},{2,34},{34,2},{3,35},{35,3},{4,36},{36... | collective-permute-start | bytes 1572872 | tf_op jit(solution)/shard_map/ppermute | solution.py:261
  134.7 14.7 %all-to-all-start.1 = ((bf16[16,144,128]{2,1,0:T(8,128)(2,1)}), bf16[16,144,128]{2,1,0:T(8,128)(2,1)S(1)}, u32[]{:S(2)}, u32[]{:S(2)}) async-start(bf16[16,144,128]{2,1,0:T(8,128)(2,1)} %get-tuple-element.33), calls=%async_computation.1 | async-start | bytes 1179648 | tf_op jit(solution)/shard_map/all_to_all | solution.py:319
  149.3 27.8 %collective-permute-start.31 = (bf16[128,2048]{1,0:T(8,128)(2,1)}, bf16[128,2048]{1,0:T(8,128)(2,1)S(1)}, u32[]{:S(2)}, u32[]{:S(2)}) collective-permute-start(bf16[128,2048]{1,0:T(8,128)(2,1)} %get-tuple-element.39), channel_id=1, source_target_pairs={{0,0},{1,1},{32,2},{33,3},{2,32},{3,33},{34,34},{35,35},{4,4},{5,5... | collective-permute-start | bytes 1572872 | tf_op jit(solution)/shard_map/ppermute | solution.py:277
  153.0 24.1 %collective-permute-start.32 = (bf16[128,2048]{1,0:T(8,128)(2,1)}, bf16[128,2048]{1,0:T(8,128)(2,1)S(1)}, u32[]{:S(2)}, u32[]{:S(2)}) collective-permute-start(bf16[128,2048]{1,0:T(8,128)(2,1)} %get-tuple-element.41), channel_id=1, source_target_pairs={{1,0},{0,1},{33,2},{32,3},{3,32},{2,33},{35,34},{34,35},{5,4},{4,5... | collective-permute-start | bytes 1572872 | tf_op jit(solution)/shard_map/ppermute | solution.py:277
  166.2 13.7 %collective-permute-start.29 = (bf16[128,2048]{1,0:T(8,128)(2,1)}, bf16[128,2048]{1,0:T(8,128)(2,1)}, u32[]{:S(2)}, u32[]{:S(2)}) collective-permute-start(bf16[128,2048]{1,0:T(8,128)(2,1)} %get-tuple-element.35), channel_id=1, source_target_pairs={{0,0},{1,1},{32,2},{33,3},{2,32},{3,33},{34,34},{35,35},{4,4},{5,5... | collective-permute-start | bytes 1572872 | tf_op jit(solution)/shard_map/ppermute | solution.py:277
  168.3 16.6 %collective-permute-start.30 = (bf16[128,2048]{1,0:T(8,128)(2,1)}, bf16[128,2048]{1,0:T(8,128)(2,1)}, u32[]{:S(2)}, u32[]{:S(2)}) collective-permute-start(bf16[128,2048]{1,0:T(8,128)(2,1)} %get-tuple-element.36), channel_id=1, source_target_pairs={{1,0},{0,1},{33,2},{32,3},{3,32},{2,33},{35,34},{34,35},{5,4},{4,5... | collective-permute-start | bytes 1572872 | tf_op jit(solution)/shard_map/ppermute | solution.py:277
  168.4 21.5 %all-to-all-start.2 = ((f32[256,1,128]{2,1,0:T(1,128)}), f32[256,1,128]{2,1,0:T(1,128)S(1)}, u32[]{:S(2)}, u32[]{:S(2)}) async-start(f32[256,1,128]{2,1,0:T(1,128)} %bitcast.63), calls=%async_computation.2 | async-start | bytes 262144 | tf_op jit(solution)/shard_map/all_to_all | solution.py:322
  (31 other events, 520.6 us)
where the time goes:
time: 193 us; the launch traced here: 192 us
  waiting for transfers between devices  83.8 us (43%)
  starting transfers between devices  54 us (28%)
  Pallas kernels  25.5 us (13%)
  blocking collectives  15.5 us (8%)
  other arithmetic  7.72 us (4%)
  local copies, waits for them, and re-layouts  3.74 us (2%)
    ppermute x10, waiting for transfers between devices, shift(): return lax.ppermute(v, 'x', [(i, (i + by) % 4) for i in range(4)])  31.4 us
    pallas_call x3, Pallas kernels, call(): pl.pallas_call(kernel, out_shape=outs, in_specs=[INS] + [INV] * (len(vmem...  25.5 us
    ppermute x15, waiting for transfers between devices, swap(): return lax.ppermute(v, axis, [(0, 1), (1, 0)])  17.8 us
    ppermute x4, waiting for transfers between devices, there(): return lax.ppermute(v, ('c', 'y'), route(k))  16.6 us
    all_to_all x1, blocking collectives, body(): hcols = lax.all_to_all(half, group, split_axis=0, concat_axis=0, tiled=True)  15.5 us
    ppermute x4, starting transfers between devices, home(): return lax.ppermute(v, ('c', 'y'), [(b, a) for a, b in route(k)])  11.3 us
    ppermute x4, starting transfers between devices, there(): return lax.ppermute(v, ('c', 'y'), route(k))  11 us
    all_to_all x1, waiting for transfers between devices, body(): brows = lax.all_to_all(back, group, split_axis=0, concat_axis=0, tiled=True)  10.6 us
  transfers between devices with their start and end apart: 35, of which 19 were waited for; matrix products, arithmetic and copies ran while one was open for 3% of the time, Pallas kernels for 4%

commit v1 on v0

--- a/solution.py
+++ b/solution.py
@@ -143,14 +143,15 @@
     gs, power_r = args[2:4], args[4]
     out, home0, home1, power, basis, lhs, acc, mom, dire, norm, right, sems = args[-12:]
     rows = load_rows(pos, gs, ((2, R),), lhs, sems)
+    rows.append(pltpu.make_async_copy(power_r, right, sems.at[42]))
+    rows[-1].start()
     groups = start_loads(pos, LEFT, args[5:-12], basis, sems)
     later = load_rows(pos, gs, ((3, 0), (4, R)), mom, sems, 34)
-    later.append(pltpu.make_async_copy(power_r, right, sems.at[42]))
-    later[-1].start()
     for i in range(16):
         lhs[:R, i * R : (i + 1) * R] = hcols[i, :R, :].astype(F32).T.astype(BF)
     for cp in rows:
         cp.wait()
+    refresh(hcols, right, norm, (home0, home1))
     multiply(groups, lhs, basis, acc)
     stores = store_rows(pos, acc, R, (power.at[:C], power.at[C:]), sems, 40)
     for cp in later:
@@ -165,7 +166,6 @@
     o0, o1 = offsets(pos)
     home0[:C, :] = (acc[pl.ds(o0, C), :] * ROOT).astype(BF)
     home1[:C, :] = (acc[pl.ds(o1, C), :] * ROOT).astype(BF)
-    refresh(hcols, right, norm, (home0, home1))
     pack_sums(acc[R:, :], norm, out)
 
     @pl.loop(0, 2)
@@ -182,11 +182,13 @@
 def raw_kernel(*args):
     pos, brows, power_l = args[:3]
     home0, home1, total, basis, lhs, raw, left, norm, sems = args[-9:]
-    groups = start_loads(pos, RIGHT, args[3:-9], basis, sems)
     power = pltpu.make_async_copy(power_l, left, sems.at[42])
     power.start()
+    groups = start_loads(pos, RIGHT, args[3:-9], basis, sems)
     for i in range(16):
         lhs[:, i * R : (i + 1) * R] = brows[i, :R, :]
+    power.wait()
+    refresh(brows, left, norm, (home0, home1))
     tot = jnp.zeros((1, X), F32)
     for xoff, copies in groups:
         for cp in copies:
@@ -199,8 +201,6 @@
     o0, o1 = offsets(pos)
     home0[:C, :] = raw[pl.ds(o0, C), :]
     home1[:C, :] = raw[pl.ds(o1, C), :]
-    power.wait()
-    refresh(brows, left, norm, (home0, home1))
     total[...] = jnp.broadcast_to(jnp.sum(tot, axis=1, keepdims=True), (256, 128))
 
 
@@ -310,7 +310,10 @@
     v_all_z = swap(v_all, "zl")
     far = [shift(after(u_near[0], *uz_near), 1), shift(after(uz_near[1], u_near[0]), -1)]
     pieces = [u, uz, *u_near, *uz_near, *far, v, vz, v_all, v_all_z]
-    pieces += other_core(*pieces[:-1], after(v_all_z, *far))
+    c_early = other_core(u, uz, *u_near)
+    c_late = other_core(*uz_near, *far)
+    v_early = other_core(v, vz)
+    pieces += c_early + c_late + v_early + other_core(v_all, after(v_all_z, *far, *c_early, *v_early))
 
     group = ("x", "zl", "c")
     half, power_r = call_half(pos, rest, pieces)

time: 193 us -> 189 us (0.979)
  waiting for transfers between devices: 83.8 us -> 80.3 us
where the time goes in v1:
time: 189 us; the launch traced here: 188 us
  waiting for transfers between devices  80.3 us (42%)
  starting transfers between devices  54 us (29%)
  Pallas kernels  25.8 us (14%)
  blocking collectives  15.8 us (8%)
  other arithmetic  7.72 us (4%)
  local copies, waits for them, and re-layouts  2.61 us (1%)
    ppermute x10, waiting for transfers between devices, shift(): return lax.ppermute(v, 'x', [(i, (i + by) % 4) for i in range(4)])  31.3 us
    pallas_call x3, Pallas kernels, call(): pl.pallas_call(kernel, out_shape=outs, in_specs=[INS] + [INV] * (len(vmem...  25.8 us
    ppermute x15, waiting for transfers between devices, swap(): return lax.ppermute(v, axis, [(0, 1), (1, 0)])  16.2 us
    all_to_all x1, blocking collectives, body(): hcols = lax.all_to_all(half, group, split_axis=0, concat_axis=0, tiled=True)  15.8 us
    ppermute x4, waiting for transfers between devices, there(): return lax.ppermute(v, ('c', 'y'), route(k))  14.9 us
    ppermute x4, starting transfers between devices, there(): return lax.ppermute(v, ('c', 'y'), route(k))  11 us
    ppermute x4, starting transfers between devices, home(): return lax.ppermute(v, ('c', 'y'), [(b, a) for a, b in route(k)])  10.8 us
    all_to_all x1, waiting for transfers between devices, body(): brows = lax.all_to_all(back, group, split_axis=0, concat_axis=0, tiled=True)  10.6 us
  transfers between devices with their start and end apart: 35, of which 19 were waited for; matrix products, arithmetic and copies ran while one was open for 3% of the time, Pallas kernels for 4%

profile of v1, /device:TPU:1, one launch (start us, length us, event | category | flops | bytes accessed | tf_op | source)
XLA Modules:
  0.0 188.0 jit_solution(9198120395507239840)
XLA Ops:
  2.0 4.2 %collective-permute-start.1 = (bf16[128,2048]{1,0:T(8,128)(2,1)S(1)}, bf16[128,2048]{1,0:T(8,128)(2,1)S(1)}, u32[]{:S(2)}, u32[]{:S(2)}) collective-permute-start(bf16[128,2048]{1,0:T(8,128)(2,1)S(1)} %pad_maximum_fusion.1), channel_id=1, source_target_pairs={{0,1},{1,0},{2,33},{3,32},{32,3},{33,2},{34,35},{35,34},{4,5},{5,4... | collective-permute-start | bytes 1572872 | tf_op jit(solution)/shard_map/ppermute | solution.py:273
  6.3 2.2 %collective-permute-start = (bf16[128,2048]{1,0:T(8,128)(2,1)S(1)}, bf16[128,2048]{1,0:T(8,128)(2,1)S(1)}, u32[]{:S(2)}, u32[]{:S(2)}) collective-permute-start(bf16[128,2048]{1,0:T(8,128)(2,1)S(1)} %pad_maximum_fusion), channel_id=1, source_target_pairs={{0,0},{1,1},{2,32},{3,33},{32,2},{33,3},{34,34},{35,35},{4,4},{5,5... | collective-permute-start | bytes 1572872 | tf_op jit(solution)/shard_map/ppermute | solution.py:273
  8.7 6.6 %collective-permute-done.1.args_11_.args_13_ = bf16[128,2048]{1,0:T(8,128)(2,1)S(1)} collective-permute-done((bf16[128,2048]{1,0:T(8,128)(2,1)S(1)}, bf16[128,2048]{1,0:T(8,128)(2,1)S(1)}, u32[]{:S(2)}, u32[]{:S(2)}) %collective-permute-start.1) | collective-permute-done | bytes 524320 | tf_op jit(solution)/shard_map/ppermute | solution.py:273
  15.3 4.8 %collective-permute-done.args_3_.args_5_ = bf16[128,2048]{1,0:T(8,128)(2,1)S(1)} collective-permute-done((bf16[128,2048]{1,0:T(8,128)(2,1)S(1)}, bf16[128,2048]{1,0:T(8,128)(2,1)S(1)}, u32[]{:S(2)}, u32[]{:S(2)}) %collective-permute-start) | collective-permute-done | bytes 524320 | tf_op jit(solution)/shard_map/ppermute | solution.py:273
  20.5 3.0 %collective-permute-start.2 = (bf16[320,2048]{1,0:T(8,128)(2,1)S(1)}, bf16[320,2048]{1,0:T(8,128)(2,1)S(1)}, u32[]{:S(2)}, u32[]{:S(2)}) collective-permute-start(bf16[320,2048]{1,0:T(8,128)(2,1)S(1)} %get-tuple-element.46), channel_id=1, source_target_pairs={{0,0},{1,1},{2,32},{3,33},{32,2},{33,3},{34,34},{35,35},{4,4},{5,5... | collective-permute-start | bytes 3932168 | tf_op jit(solution)/shard_map/ppermute | solution.py:273
  23.5 1.5 collective-permute-start.3
  26.2 1.5 collective-permute-start.13
  27.7 1.6 collective-permute-start.4
  29.3 6.1 %collective-permute-done.12 = bf16[128,2048]{1,0:T(8,128)(2,1)S(1)} collective-permute-done((bf16[128,2048]{1,0:T(8,128)(2,1)S(1)}, bf16[128,2048]{1,0:T(8,128)(2,1)S(1)}, u32[]{:S(2)}, u32[]{:S(2)}) %collective-permute-start.12) | collective-permute-done | bytes 524320 | tf_op jit(solution)/shard_map/ppermute | solution.py:253
  36.5 2.7 %collective-permute-start.11 = (bf16[128,2048]{1,0:T(8,128)(2,1)S(1)}, bf16[128,2048]{1,0:T(8,128)(2,1)S(1)}, u32[]{:S(2)}, u32[]{:S(2)}) collective-permute-start(bf16[128,2048]{1,0:T(8,128)(2,1)S(1)} %collective-permute-done.1.args_11_.args_13_), channel_id=1, source_target_pairs={{0,4},{4,0},{1,5},{5,1},{2,6},{6,2},{3,7},{7,3},{8,12},{12,8},{9,1... | collective-permute-start | bytes 1572872 | tf_op jit(solution)/shard_map/ppermute | solution.py:261
  40.8 5.4 %collective-permute-done.5.args_5_.args_7_ = bf16[128,2048]{1,0:T(8,128)(2,1)S(1)} collective-permute-done((bf16[128,2048]{1,0:T(8,128)(2,1)S(1)}, bf16[128,2048]{1,0:T(8,128)(2,1)S(1)}, u32[]{:S(2)}, u32[]{:S(2)}) %collective-permute-start.5) | collective-permute-done | bytes 524320 | tf_op jit(solution)/shard_map/ppermute | solution.py:253
  50.7 1.7 collective-permute-start.7
  52.4 3.4 %collective-permute-done.3.args_2_.args_3_ = bf16[320,2048]{1,0:T(8,128)(2,1)} collective-permute-done((bf16[320,2048]{1,0:T(8,128)(2,1)S(1)}, bf16[320,2048]{1,0:T(8,128)(2,1)}, u32[]{:S(2)}, u32[]{:S(2)}) %collective-permute-start.3) | collective-permute-done | bytes 1310752 | tf_op jit(solution)/shard_map/ppermute | solution.py:273
  58.9 7.0 %collective-permute-done.8.args_8_.args_10_ = bf16[128,2048]{1,0:T(8,128)(2,1)S(1)} collective-permute-done((bf16[128,2048]{1,0:T(8,128)(2,1)S(1)}, bf16[128,2048]{1,0:T(8,128)(2,1)S(1)}, u32[]{:S(2)}, u32[]{:S(2)}) %collective-permute-start.8) | collective-permute-done | bytes 524320 | tf_op jit(solution)/shard_map/ppermute | solution.py:253
  68.6 1.9 %collective-permute-start.10 = (bf16[128,2048]{1,0:T(8,128)(2,1)S(1)}, bf16[128,2048]{1,0:T(8,128)(2,1)}, u32[]{:S(2)}, u32[]{:S(2)}) collective-permute-start(bf16[128,2048]{1,0:T(8,128)(2,1)S(1)} %collective-permute-done.8.args_8_.args_10_), channel_id=1, source_target_pairs={{0,24},{8,0},{16,8},{24,16},{1,25},{9,1},{17,9},{25,17},{2,26},{10... | collective-permute-start | bytes 1572872 | tf_op jit(solution)/shard_map/ppermute | solution.py:253
  71.2 11.3 %collective-permute-done.9.args_9_.args_11_ = bf16[128,2048]{1,0:T(8,128)(2,1)} collective-permute-done((bf16[128,2048]{1,0:T(8,128)(2,1)S(1)}, bf16[128,2048]{1,0:T(8,128)(2,1)}, u32[]{:S(2)}, u32[]{:S(2)}) %collective-permute-start.9) | collective-permute-done | bytes 524320 | tf_op jit(solution)/shard_map/ppermute | solution.py:253
  82.5 7.0 %collective-permute-done.16.args_14_.args_16_ = bf16[384,2048]{1,0:T(8,128)(2,1)S(1)} collective-permute-done((bf16[384,2048]{1,0:T(8,128)(2,1)S(1)}, bf16[384,2048]{1,0:T(8,128)(2,1)S(1)}, u32[]{:S(2)}, u32[]{:S(2)}) %collective-permute-start.16) | collective-permute-done | bytes 1572896 | tf_op jit(solution)/shard_map/ppermute | solution.py:261
  90.6 3.5 %collective-permute-done.22.args_20_.args_22_ = bf16[128,2048]{1,0:T(8,128)(2,1)S(1)} collective-permute-done((bf16[128,2048]{1,0:T(8,128)(2,1)S(1)}, bf16[128,2048]{1,0:T(8,128)(2,1)S(1)}, u32[]{:S(2)}, u32[]{:S(2)}) %collective-permute-start.22) | collective-permute-done | bytes 524320 | tf_op jit(solution)/shard_map/ppermute | solution.py:261
  97.2 7.2 %half.1 = (bf16[16,144,128]{2,1,0:T(8,128)(2,1)}, f32[128,2048]{1,0:T(8,128)}) custom-call(s32[4]{0:T(128)} %pad_add_fusion.args_0_, bf16[320,2048]{1,0:T(8,128)(2,1)} %copy-done.2, bf16[320,2048]{1,0:T(8,128)(2,1)} %collective-permute-done.3.args_2_.args_3_, bf16[128,2048]{1,0:T(8,128)(2,1)} %copy-done.4, bf16[128,2048]{1,0:T(8,128)(2,1)} %copy-done.5, ...), custom_call_target="tpu_custom_call" | custom-call | flops 2147483648 | bytes 12582912 | tf_op jit(solution)/shard_map/half/pallas_call | solution.py:212
  104.4 15.8 %all_to_all.22.args_1_ = bf16[16,144,128]{2,1,0:T(8,128)(2,1)} all-to-all(bf16[16,144,128]{2,1,0:T(8,128)(2,1)} %get-tuple-element.31), channel_id=1, replica_groups=mesh['zh'=4,'c'=2,'x'=4,'zl'=2,'y'=4] {'x','zl','c'}, dimensions={0} | all-to-all | bytes 1179648 | tf_op jit(solution)/shard_map/all_to_all | solution.py:320
  120.2 10.7 %left.1 = (bf16[16,144,128]{2,1,0:T(8,128)(2,1)}, bf16[128,2048]{1,0:T(8,128)(2,1)}, bf16[128,2048]{1,0:T(8,128)(2,1)}, f32[128,2048]{1,0:T(8,128)}) custom-call(s32[4]{0:T(128)} %pad_add_fusion.args_0_, bf16[16,144,128]{2,1,0:T(8,128)(2,1)} %all_to_all.22.args_1_, bf16[320,2048]{1,0:T(8,128)(2,1)} %copy-done.2, ...), custom_call_target="tpu_custom_call" | custom-call | flops 3221225472 | bytes 12582912 | tf_op jit(solution)/shard_map/left/pallas_call | solution.py:212
  130.9 4.0 %all-to-all-start.1 = ((bf16[16,144,128]{2,1,0:T(8,128)(2,1)}), bf16[16,144,128]{2,1,0:T(8,128)(2,1)S(1)}, u32[]{:S(2)}, u32[]{:S(2)}) async-start(bf16[16,144,128]{2,1,0:T(8,128)(2,1)} %get-tuple-element.33), calls=%async_computation.1 | async-start | bytes 1179648 | tf_op jit(solution)/shard_map/all_to_all | solution.py:322
  135.0 10.6 %all-to-all-done.1.args_1_ = bf16[16,144,128]{2,1,0:T(8,128)(2,1)S(1)} async-done(((bf16[16,144,128]{2,1,0:T(8,128)(2,1)}), bf16[16,144,128]{2,1,0:T(8,128)(2,1)S(1)}, u32[]{:S(2)}, u32[]{:S(2)}) %all-to-all-start.1) | async-done | bytes 589856 | tf_op jit(solution)/shard_map/all_to_all | solution.py:322
  145.6 3.9 %collective-permute-start.31 = (bf16[128,2048]{1,0:T(8,128)(2,1)}, bf16[128,2048]{1,0:T(8,128)(2,1)S(1)}, u32[]{:S(2)}, u32[]{:S(2)}) collective-permute-start(bf16[128,2048]{1,0:T(8,128)(2,1)} %get-tuple-element.39), channel_id=1, source_target_pairs={{0,0},{1,1},{32,2},{33,3},{2,32},{3,33},{34,34},{35,35},{4,4},{5,5... | collective-permute-start | bytes 1572872 | tf_op jit(solution)/shard_map/ppermute | solution.py:277
  149.5 4.7 %collective-permute-start.32 = (bf16[128,2048]{1,0:T(8,128)(2,1)}, bf16[128,2048]{1,0:T(8,128)(2,1)S(1)}, u32[]{:S(2)}, u32[]{:S(2)}) collective-permute-start(bf16[128,2048]{1,0:T(8,128)(2,1)} %get-tuple-element.41), channel_id=1, source_target_pairs={{1,0},{0,1},{33,2},{32,3},{3,32},{2,33},{35,34},{34,35},{5,4},{4,5... | collective-permute-start | bytes 1572872 | tf_op jit(solution)/shard_map/ppermute | solution.py:277
  154.2 7.9 %raw.1 = (bf16[128,2048]{1,0:T(8,128)(2,1)}, bf16[128,2048]{1,0:T(8,128)(2,1)}, f32[256,128]{1,0:T(8,128)}) custom-call(s32[4]{0:T(128)} %pad_add_fusion.args_0_, bf16[16,144,128]{2,1,0:T(8,128)(2,1)} %copy-done.21, f32[128,2048]{1,0:T(8,128)} %get-tuple-element.34.args_2_, bf16[128,2048]{1,0:T(8,128)(2,1)} %copy-done.4, bf16[128,2048]{1,0:T(8,128)(2,1)} %copy-done.5, ...), custom_call_target="tpu_custom_call" | custom-call | flops 1073741824 | bytes 12582912 | tf_op jit(solution)/shard_map/raw/pallas_call | solution.py:212
  162.1 2.1 %collective-permute-start.29 = (bf16[128,2048]{1,0:T(8,128)(2,1)}, bf16[128,2048]{1,0:T(8,128)(2,1)}, u32[]{:S(2)}, u32[]{:S(2)}) collective-permute-start(bf16[128,2048]{1,0:T(8,128)(2,1)} %get-tuple-element.35), channel_id=1, source_target_pairs={{0,0},{1,1},{32,2},{33,3},{2,32},{3,33},{34,34},{35,35},{4,4},{5,5... | collective-permute-start | bytes 1572872 | tf_op jit(solution)/shard_map/ppermute | solution.py:277
  164.3 8.8 %all-to-all-start.2 = ((f32[256,1,128]{2,1,0:T(1,128)}), f32[256,1,128]{2,1,0:T(1,128)S(1)}, u32[]{:S(2)}, u32[]{:S(2)}) async-start(f32[256,1,128]{2,1,0:T(1,128)} %bitcast.63), calls=%async_computation.2 | async-start | bytes 262144 | tf_op jit(solution)/shard_map/all_to_all | solution.py:325
  173.3 1.6 fusion.3
  175.8 4.9 %collective-permute-done.30 = bf16[128,2048]{1,0:T(8,128)(2,1)} collective-permute-done((bf16[128,2048]{1,0:T(8,128)(2,1)}, bf16[128,2048]{1,0:T(8,128)(2,1)}, u32[]{:S(2)}, u32[]{:S(2)}) %collective-permute-start.30) | collective-permute-done | bytes 524320 | tf_op jit(solution)/shard_map/ppermute | solution.py:277
  180.7 1.7 maximum_select_fusion
  183.3 2.5 %all-to-all-done.2 = f32[256,1,128]{2,1,0:T(1,128)S(1)} async-done(((f32[256,1,128]{2,1,0:T(1,128)}), f32[256,1,128]{2,1,0:T(1,128)S(1)}, u32[]{:S(2)}, u32[]{:S(2)}) %all-to-all-start.2) | async-done | bytes 131104 | tf_op jit(solution)/shard_map/all_to_all | solution.py:325
  (124 shorter events, 24.3 us)
Async XLA Ops:
  2.0 13.3 %collective-permute-start.1 = (bf16[128,2048]{1,0:T(8,128)(2,1)S(1)}, bf16[128,2048]{1,0:T(8,128)(2,1)S(1)}, u32[]{:S(2)}, u32[]{:S(2)}) collective-permute-start(bf16[128,2048]{1,0:T(8,128)(2,1)S(1)} %pad_maximum_fusion.1), channel_id=1, source_target_pairs={{0,1},{1,0},{2,33},{3,32},{32,3},{33,2},{34,35},{35,34},{4,5},{5,4... | collective-permute-start | bytes 1572872 | tf_op jit(solution)/shard_map/ppermute | solution.py:273
  6.3 13.9 %collective-permute-start = (bf16[128,2048]{1,0:T(8,128)(2,1)S(1)}, bf16[128,2048]{1,0:T(8,128)(2,1)S(1)}, u32[]{:S(2)}, u32[]{:S(2)}) collective-permute-start(bf16[128,2048]{1,0:T(8,128)(2,1)S(1)} %pad_maximum_fusion), channel_id=1, source_target_pairs={{0,0},{1,1},{2,32},{3,33},{32,2},{33,3},{34,34},{35,35},{4,4},{5,5... | collective-permute-start | bytes 1572872 | tf_op jit(solution)/shard_map/ppermute | solution.py:273
  20.5 30.3 %collective-permute-start.2 = (bf16[320,2048]{1,0:T(8,128)(2,1)S(1)}, bf16[320,2048]{1,0:T(8,128)(2,1)S(1)}, u32[]{:S(2)}, u32[]{:S(2)}) collective-permute-start(bf16[320,2048]{1,0:T(8,128)(2,1)S(1)} %get-tuple-element.46), channel_id=1, source_target_pairs={{0,0},{1,1},{2,32},{3,33},{32,2},{33,3},{34,34},{35,35},{4,4},{5,5... | collective-permute-start | bytes 3932168 | tf_op jit(solution)/shard_map/ppermute | solution.py:273
  23.5 32.4 %collective-permute-start.3 = (bf16[320,2048]{1,0:T(8,128)(2,1)S(1)}, bf16[320,2048]{1,0:T(8,128)(2,1)}, u32[]{:S(2)}, u32[]{:S(2)}) collective-permute-start(bf16[320,2048]{1,0:T(8,128)(2,1)S(1)} %get-tuple-element.45), channel_id=1, source_target_pairs={{0,1},{1,0},{2,33},{3,32},{32,3},{33,2},{34,35},{35,34},{4,5},{5,4... | collective-permute-start | bytes 3932168 | tf_op jit(solution)/shard_map/ppermute | solution.py:273
  25.0 10.4 %collective-permute-start.12 = (bf16[128,2048]{1,0:T(8,128)(2,1)S(1)}, bf16[128,2048]{1,0:T(8,128)(2,1)S(1)}, u32[]{:S(2)}, u32[]{:S(2)}) collective-permute-start(bf16[128,2048]{1,0:T(8,128)(2,1)S(1)} %collective-permute-done.1.args_11_.args_13_), channel_id=1, source_target_pairs={{0,8},{8,16},{16,24},{24,0},{1,9},{9,17},{17,25},{25,1},{2,10},{10... | collective-permute-start | bytes 1572872 | tf_op jit(solution)/shard_map/ppermute | solution.py:253
  26.2 10.3 %collective-permute-start.13 = (bf16[128,2048]{1,0:T(8,128)(2,1)S(1)}, bf16[128,2048]{1,0:T(8,128)(2,1)S(1)}, u32[]{:S(2)}, u32[]{:S(2)}) collective-permute-start(bf16[128,2048]{1,0:T(8,128)(2,1)S(1)} %collective-permute-done.1.args_11_.args_13_), channel_id=1, source_target_pairs={{0,24},{8,0},{16,8},{24,16},{1,25},{9,1},{17,9},{25,17},{2,26},{10... | collective-permute-start | bytes 1572872 | tf_op jit(solution)/shard_map/ppermute | solution.py:253
  27.7 13.1 %collective-permute-start.4 = (bf16[128,2048]{1,0:T(8,128)(2,1)S(1)}, bf16[128,2048]{1,0:T(8,128)(2,1)S(1)}, u32[]{:S(2)}, u32[]{:S(2)}) collective-permute-start(bf16[128,2048]{1,0:T(8,128)(2,1)S(1)} %collective-permute-done.args_3_.args_5_), channel_id=1, source_target_pairs={{0,4},{4,0},{1,5},{5,1},{2,6},{6,2},{3,7},{7,3},{8,12},{12,8},{9,1... | collective-permute-start | bytes 1572872 | tf_op jit(solution)/shard_map/ppermute | solution.py:261
  35.4 10.9 %collective-permute-start.5 = (bf16[128,2048]{1,0:T(8,128)(2,1)S(1)}, bf16[128,2048]{1,0:T(8,128)(2,1)S(1)}, u32[]{:S(2)}, u32[]{:S(2)}) collective-permute-start(bf16[128,2048]{1,0:T(8,128)(2,1)S(1)} %collective-permute-done.args_3_.args_5_), channel_id=1, source_target_pairs={{0,8},{8,16},{16,24},{24,0},{1,9},{9,17},{17,25},{25,1},{2,10},{10... | collective-permute-start | bytes 1572872 | tf_op jit(solution)/shard_map/ppermute | solution.py:253
  36.5 12.0 %collective-permute-start.11 = (bf16[128,2048]{1,0:T(8,128)(2,1)S(1)}, bf16[128,2048]{1,0:T(8,128)(2,1)S(1)}, u32[]{:S(2)}, u32[]{:S(2)}) collective-permute-start(bf16[128,2048]{1,0:T(8,128)(2,1)S(1)} %collective-permute-done.1.args_11_.args_13_), channel_id=1, source_target_pairs={{0,4},{4,0},{1,5},{5,1},{2,6},{6,2},{3,7},{7,3},{8,12},{12,8},{9,1... | collective-permute-start | bytes 1572872 | tf_op jit(solution)/shard_map/ppermute | solution.py:261
  40.7 8.5 %collective-permute-start.6 = (bf16[128,2048]{1,0:T(8,128)(2,1)S(1)}, bf16[128,2048]{1,0:T(8,128)(2,1)S(1)}, u32[]{:S(2)}, u32[]{:S(2)}) collective-permute-start(bf16[128,2048]{1,0:T(8,128)(2,1)S(1)} %collective-permute-done.args_3_.args_5_), channel_id=1, source_target_pairs={{0,24},{8,0},{16,8},{24,16},{1,25},{9,1},{17,9},{25,17},{2,26},{10... | collective-permute-start | bytes 1572872 | tf_op jit(solution)/shard_map/ppermute | solution.py:253
  46.2 9.7 %collective-permute-start.14 = (bf16[64,2048]{1,0:T(8,128)(2,1)S(1)}, bf16[64,2048]{1,0:T(8,128)(2,1)S(1)}, u32[]{:S(2)}, u32[]{:S(2)}) collective-permute-start(bf16[64,2048]{1,0:T(8,128)(2,1)S(1)} %slice.36), channel_id=1, source_target_pairs={{0,8},{8,16},{16,24},{24,0},{1,9},{9,17},{17,25},{25,1},{2,10},{10... | collective-permute-start | bytes 786440 | tf_op jit(solution)/shard_map/ppermute | solution.py:253
  48.5 8.5 %collective-permute-start.15 = (bf16[64,2048]{1,0:T(8,128)(2,1)S(1)}, bf16[64,2048]{1,0:T(8,128)(2,1)S(1)}, u32[]{:S(2)}, u32[]{:S(2)}) collective-permute-start(bf16[64,2048]{1,0:T(8,128)(2,1)S(1)} %slice.37), channel_id=1, source_target_pairs={{0,24},{8,0},{16,8},{24,16},{1,25},{9,1},{17,9},{25,17},{2,26},{10... | collective-permute-start | bytes 786440 | tf_op jit(solution)/shard_map/ppermute | solution.py:253
  49.3 16.6 %collective-permute-start.8 = (bf16[128,2048]{1,0:T(8,128)(2,1)S(1)}, bf16[128,2048]{1,0:T(8,128)(2,1)S(1)}, u32[]{:S(2)}, u32[]{:S(2)}) collective-permute-start(bf16[128,2048]{1,0:T(8,128)(2,1)S(1)} %collective-permute-done.4.args_4_.args_6_), channel_id=1, source_target_pairs={{0,24},{8,0},{16,8},{24,16},{1,25},{9,1},{17,9},{25,17},{2,26},{10... | collective-permute-start | bytes 1572872 | tf_op jit(solution)/shard_map/ppermute | solution.py:253
  50.7 15.2 %collective-permute-start.7 = (bf16[128,2048]{1,0:T(8,128)(2,1)S(1)}, bf16[128,2048]{1,0:T(8,128)(2,1)}, u32[]{:S(2)}, u32[]{:S(2)}) collective-permute-start(bf16[128,2048]{1,0:T(8,128)(2,1)S(1)} %collective-permute-done.4.args_4_.args_6_), channel_id=1, source_target_pairs={{0,8},{8,16},{16,24},{24,0},{1,9},{9,17},{17,25},{25,1},{2,10},{10... | collective-permute-start | bytes 1572872 | tf_op jit(solution)/shard_map/ppermute | solution.py:253
  57.1 32.4 %collective-permute-start.16 = (bf16[384,2048]{1,0:T(8,128)(2,1)S(1)}, bf16[384,2048]{1,0:T(8,128)(2,1)S(1)}, u32[]{:S(2)}, u32[]{:S(2)}) collective-permute-start(bf16[384,2048]{1,0:T(8,128)(2,1)S(1)} %constant_dynamic-update-slice_fusion.args_13_.args_15_), channel_id=1, source_target_pairs={{0,4},{4,0},{1,5},{5,1},{2,6},{6,2},{3,7},{7,3},{8,12},{12,8},{9,1... | collective-permute-start | bytes 4718600 | tf_op jit(solution)/shard_map/ppermute | solution.py:261
  58.4 8.1 %collective-permute-start.25 = (bf16[128,2048]{1,0:T(8,128)(2,1)S(1)}, bf16[128,2048]{1,0:T(8,128)(2,1)S(1)}, u32[]{:S(2)}, u32[]{:S(2)}) collective-permute-start(bf16[128,2048]{1,0:T(8,128)(2,1)S(1)} %collective-permute-done.1.args_11_.args_13_), channel_id=1, source_target_pairs={{0,32},{32,0},{1,33},{33,1},{2,34},{34,2},{3,35},{35,3},{4,36},{36... | collective-permute-start | bytes 1572872 | tf_op jit(solution)/shard_map/ppermute | solution.py:261
  58.4 8.3 %collective-permute-start.17 = (bf16[128,2048]{1,0:T(8,128)(2,1)S(1)}, bf16[128,2048]{1,0:T(8,128)(2,1)S(1)}, u32[]{:S(2)}, u32[]{:S(2)}) collective-permute-start(bf16[128,2048]{1,0:T(8,128)(2,1)S(1)} %collective-permute-done.args_3_.args_5_), channel_id=1, source_target_pairs={{0,32},{32,0},{1,33},{33,1},{2,34},{34,2},{3,35},{35,3},{4,36},{36... | collective-permute-start | bytes 1572872 | tf_op jit(solution)/shard_map/ppermute | solution.py:261
  66.4 4.1 %collective-permute-start.26 = (bf16[128,2048]{1,0:T(8,128)(2,1)S(1)}, bf16[128,2048]{1,0:T(8,128)(2,1)S(1)}, u32[]{:S(2)}, u32[]{:S(2)}) collective-permute-start(bf16[128,2048]{1,0:T(8,128)(2,1)S(1)} %collective-permute-done.11.args_12_.args_14_), channel_id=1, source_target_pairs={{0,32},{32,0},{1,33},{33,1},{2,34},{34,2},{3,35},{35,3},{4,36},{36... | collective-permute-start | bytes 1572872 | tf_op jit(solution)/shard_map/ppermute | solution.py:261
  66.7 4.5 %collective-permute-start.20 = (bf16[128,2048]{1,0:T(8,128)(2,1)S(1)}, bf16[128,2048]{1,0:T(8,128)(2,1)S(1)}, u32[]{:S(2)}, u32[]{:S(2)}) collective-permute-start(bf16[128,2048]{1,0:T(8,128)(2,1)S(1)} %collective-permute-done.6.args_6_.args_8_), channel_id=1, source_target_pairs={{0,32},{32,0},{1,33},{33,1},{2,34},{34,2},{3,35},{35,3},{4,36},{36... | collective-permute-start | bytes 1572872 | tf_op jit(solution)/shard_map/ppermute | solution.py:261
  67.8 14.7 %collective-permute-start.9 = (bf16[128,2048]{1,0:T(8,128)(2,1)S(1)}, bf16[128,2048]{1,0:T(8,128)(2,1)}, u32[]{:S(2)}, u32[]{:S(2)}) collective-permute-start(bf16[128,2048]{1,0:T(8,128)(2,1)S(1)} %collective-permute-done.5.args_5_.args_7_), channel_id=1, source_target_pairs={{0,8},{8,16},{16,24},{24,0},{1,9},{9,17},{17,25},{25,1},{2,10},{10... | collective-permute-start | bytes 1572872 | tf_op jit(solution)/shard_map/ppermute | solution.py:253
  68.6 14.0 %collective-permute-start.10 = (bf16[128,2048]{1,0:T(8,128)(2,1)S(1)}, bf16[128,2048]{1,0:T(8,128)(2,1)}, u32[]{:S(2)}, u32[]{:S(2)}) collective-permute-start(bf16[128,2048]{1,0:T(8,128)(2,1)S(1)} %collective-permute-done.8.args_8_.args_10_), channel_id=1, source_target_pairs={{0,24},{8,0},{16,8},{24,16},{1,25},{9,1},{17,9},{25,17},{2,26},{10... | collective-permute-start | bytes 1572872 | tf_op jit(solution)/shard_map/ppermute | solution.py:253
  70.5 26.6 %collective-permute-start.27 = (bf16[384,2048]{1,0:T(8,128)(2,1)S(1)}, bf16[384,2048]{1,0:T(8,128)(2,1)}, u32[]{:S(2)}, u32[]{:S(2)}) collective-permute-start(bf16[384,2048]{1,0:T(8,128)(2,1)S(1)} %constant_dynamic-update-slice_fusion.args_13_.args_15_), channel_id=1, source_target_pairs={{0,32},{32,0},{1,33},{33,1},{2,34},{34,2},{3,35},{35,3},{4,36},{36... | collective-permute-start | bytes 4718600 | tf_op jit(solution)/shard_map/ppermute | solution.py:261
  89.5 7.6 %collective-permute-start.28 = (bf16[384,2048]{1,0:T(8,128)(2,1)S(1)}, bf16[384,2048]{1,0:T(8,128)(2,1)}, u32[]{:S(2)}, u32[]{:S(2)}) collective-permute-start(bf16[384,2048]{1,0:T(8,128)(2,1)S(1)} %collective-permute-done.16.args_14_.args_16_), channel_id=1, source_target_pairs={{0,32},{32,0},{1,33},{33,1},{2,34},{34,2},{3,35},{35,3},{4,36},{36... | collective-permute-start | bytes 4718600 | tf_op jit(solution)/shard_map/ppermute | solution.py:261
  89.5 4.5 %collective-permute-start.22 = (bf16[128,2048]{1,0:T(8,128)(2,1)S(1)}, bf16[128,2048]{1,0:T(8,128)(2,1)S(1)}, u32[]{:S(2)}, u32[]{:S(2)}) collective-permute-start(bf16[128,2048]{1,0:T(8,128)(2,1)S(1)} %collective-permute-done.8.args_8_.args_10_), channel_id=1, source_target_pairs={{0,32},{32,0},{1,33},{33,1},{2,34},{34,2},{3,35},{35,3},{4,36},{36... | collective-permute-start | bytes 1572872 | tf_op jit(solution)/shard_map/ppermute | solution.py:261
  90.0 5.9 %collective-permute-start.21 = (bf16[128,2048]{1,0:T(8,128)(2,1)}, bf16[128,2048]{1,0:T(8,128)(2,1)}, u32[]{:S(2)}, u32[]{:S(2)}) collective-permute-start(bf16[128,2048]{1,0:T(8,128)(2,1)} %collective-permute-done.7.args_7_.args_9_), channel_id=1, source_target_pairs={{0,32},{32,0},{1,33},{33,1},{2,34},{34,2},{3,35},{35,3},{4,36},{36... | collective-permute-start | bytes 1572872 | tf_op jit(solution)/shard_map/ppermute | solution.py:261
  90.1 5.8 %collective-permute-start.23 = (bf16[128,2048]{1,0:T(8,128)(2,1)}, bf16[128,2048]{1,0:T(8,128)(2,1)}, u32[]{:S(2)}, u32[]{:S(2)}) collective-permute-start(bf16[128,2048]{1,0:T(8,128)(2,1)} %collective-permute-done.9.args_9_.args_11_), channel_id=1, source_target_pairs={{0,32},{32,0},{1,33},{33,1},{2,34},{34,2},{3,35},{35,3},{4,36},{36... | collective-permute-start | bytes 1572872 | tf_op jit(solution)/shard_map/ppermute | solution.py:261
  130.9 14.7 %all-to-all-start.1 = ((bf16[16,144,128]{2,1,0:T(8,128)(2,1)}), bf16[16,144,128]{2,1,0:T(8,128)(2,1)S(1)}, u32[]{:S(2)}, u32[]{:S(2)}) async-start(bf16[16,144,128]{2,1,0:T(8,128)(2,1)} %get-tuple-element.33), calls=%async_computation.1 | async-start | bytes 1179648 | tf_op jit(solution)/shard_map/all_to_all | solution.py:322
  145.6 27.5 %collective-permute-start.31 = (bf16[128,2048]{1,0:T(8,128)(2,1)}, bf16[128,2048]{1,0:T(8,128)(2,1)S(1)}, u32[]{:S(2)}, u32[]{:S(2)}) collective-permute-start(bf16[128,2048]{1,0:T(8,128)(2,1)} %get-tuple-element.39), channel_id=1, source_target_pairs={{0,0},{1,1},{32,2},{33,3},{2,32},{3,33},{34,34},{35,35},{4,4},{5,5... | collective-permute-start | bytes 1572872 | tf_op jit(solution)/shard_map/ppermute | solution.py:277
  149.5 23.6 %collective-permute-start.32 = (bf16[128,2048]{1,0:T(8,128)(2,1)}, bf16[128,2048]{1,0:T(8,128)(2,1)S(1)}, u32[]{:S(2)}, u32[]{:S(2)}) collective-permute-start(bf16[128,2048]{1,0:T(8,128)(2,1)} %get-tuple-element.41), channel_id=1, source_target_pairs={{1,0},{0,1},{33,2},{32,3},{3,32},{2,33},{35,34},{34,35},{5,4},{4,5... | collective-permute-start | bytes 1572872 | tf_op jit(solution)/shard_map/ppermute | solution.py:277
  162.1 13.7 %collective-permute-start.29 = (bf16[128,2048]{1,0:T(8,128)(2,1)}, bf16[128,2048]{1,0:T(8,128)(2,1)}, u32[]{:S(2)}, u32[]{:S(2)}) collective-permute-start(bf16[128,2048]{1,0:T(8,128)(2,1)} %get-tuple-element.35), channel_id=1, source_target_pairs={{0,0},{1,1},{32,2},{33,3},{2,32},{3,33},{34,34},{35,35},{4,4},{5,5... | collective-permute-start | bytes 1572872 | tf_op jit(solution)/shard_map/ppermute | solution.py:277
  164.2 16.5 %collective-permute-start.30 = (bf16[128,2048]{1,0:T(8,128)(2,1)}, bf16[128,2048]{1,0:T(8,128)(2,1)}, u32[]{:S(2)}, u32[]{:S(2)}) collective-permute-start(bf16[128,2048]{1,0:T(8,128)(2,1)} %get-tuple-element.36), channel_id=1, source_target_pairs={{1,0},{0,1},{33,2},{32,3},{3,32},{2,33},{35,34},{34,35},{5,4},{4,5... | collective-permute-start | bytes 1572872 | tf_op jit(solution)/shard_map/ppermute | solution.py:277
  164.3 21.5 %all-to-all-start.2 = ((f32[256,1,128]{2,1,0:T(1,128)}), f32[256,1,128]{2,1,0:T(1,128)S(1)}, u32[]{:S(2)}, u32[]{:S(2)}) async-start(f32[256,1,128]{2,1,0:T(1,128)} %bitcast.63), calls=%async_computation.2 | async-start | bytes 262144 | tf_op jit(solution)/shard_map/all_to_all | solution.py:325
  (31 other events, 565.9 us)

commit v2 on v1

--- a/solution.py
+++ b/solution.py
@@ -14,7 +14,7 @@
 R = 128
 X = 512
 ROOT = 1.0 / math.sqrt(W)
-VMEM = 56 * 1024 * 1024
+VMEM = 60 * 1024 * 1024
 HBM = pl.BlockSpec(memory_space=pltpu.HBM)
 INV = pl.BlockSpec(memory_space=pltpu.VMEM)
 INS = pl.BlockSpec(memory_space=pltpu.SMEM)

time: 189 us -> 189 us (level)
  no operation moved by 1% of the time
where the time goes in v2:
time: 189 us; the launch traced here: 188 us
  waiting for transfers between devices  80.3 us (42%)
  starting transfers between devices  54 us (29%)
  Pallas kernels  25.8 us (14%)
  blocking collectives  15.8 us (8%)
  other arithmetic  7.72 us (4%)
  local copies, waits for them, and re-layouts  2.61 us (1%)
    ppermute x10, waiting for transfers between devices, shift(): return lax.ppermute(v, 'x', [(i, (i + by) % 4) for i in range(4)])  31.3 us
    pallas_call x3, Pallas kernels, call(): pl.pallas_call(kernel, out_shape=outs, in_specs=[INS] + [INV] * (len(vmem...  25.8 us
    ppermute x15, waiting for transfers between devices, swap(): return lax.ppermute(v, axis, [(0, 1), (1, 0)])  16.2 us
    all_to_all x1, blocking collectives, body(): hcols = lax.all_to_all(half, group, split_axis=0, concat_axis=0, tiled=True)  15.8 us
    ppermute x4, waiting for transfers between devices, there(): return lax.ppermute(v, ('c', 'y'), route(k))  14.9 us
    ppermute x4, starting transfers between devices, there(): return lax.ppermute(v, ('c', 'y'), route(k))  11 us
    ppermute x4, starting transfers between devices, home(): return lax.ppermute(v, ('c', 'y'), [(b, a) for a, b in route(k)])  10.8 us
    all_to_all x1, waiting for transfers between devices, body(): brows = lax.all_to_all(back, group, split_axis=0, concat_axis=0, tiled=True)  10.6 us
  transfers between devices with their start and end apart: 35, of which 19 were waited for; matrix products, arithmetic and copies ran while one was open for 3% of the time, Pallas kernels for 4%

profile of v2, /device:TPU:1, one launch (start us, length us, event | category | flops | bytes accessed | tf_op | source)
XLA Modules:
  0.0 188.0 jit_solution(9198120395507239840)
XLA Ops:
  2.0 4.2 %collective-permute-start.1 = (bf16[128,2048]{1,0:T(8,128)(2,1)S(1)}, bf16[128,2048]{1,0:T(8,128)(2,1)S(1)}, u32[]{:S(2)}, u32[]{:S(2)}) collective-permute-start(bf16[128,2048]{1,0:T(8,128)(2,1)S(1)} %pad_maximum_fusion.1), channel_id=1, source_target_pairs={{0,1},{1,0},{2,33},{3,32},{32,3},{33,2},{34,35},{35,34},{4,5},{5,4... | collective-permute-start | bytes 1572872 | tf_op jit(solution)/shard_map/ppermute | solution.py:273
  6.3 2.2 %collective-permute-start = (bf16[128,2048]{1,0:T(8,128)(2,1)S(1)}, bf16[128,2048]{1,0:T(8,128)(2,1)S(1)}, u32[]{:S(2)}, u32[]{:S(2)}) collective-permute-start(bf16[128,2048]{1,0:T(8,128)(2,1)S(1)} %pad_maximum_fusion), channel_id=1, source_target_pairs={{0,0},{1,1},{2,32},{3,33},{32,2},{33,3},{34,34},{35,35},{4,4},{5,5... | collective-permute-start | bytes 1572872 | tf_op jit(solution)/shard_map/ppermute | solution.py:273
  8.7 6.6 %collective-permute-done.1.args_11_.args_13_ = bf16[128,2048]{1,0:T(8,128)(2,1)S(1)} collective-permute-done((bf16[128,2048]{1,0:T(8,128)(2,1)S(1)}, bf16[128,2048]{1,0:T(8,128)(2,1)S(1)}, u32[]{:S(2)}, u32[]{:S(2)}) %collective-permute-start.1) | collective-permute-done | bytes 524320 | tf_op jit(solution)/shard_map/ppermute | solution.py:273
  15.3 4.8 %collective-permute-done.args_3_.args_5_ = bf16[128,2048]{1,0:T(8,128)(2,1)S(1)} collective-permute-done((bf16[128,2048]{1,0:T(8,128)(2,1)S(1)}, bf16[128,2048]{1,0:T(8,128)(2,1)S(1)}, u32[]{:S(2)}, u32[]{:S(2)}) %collective-permute-start) | collective-permute-done | bytes 524320 | tf_op jit(solution)/shard_map/ppermute | solution.py:273
  20.5 3.0 %collective-permute-start.2 = (bf16[320,2048]{1,0:T(8,128)(2,1)S(1)}, bf16[320,2048]{1,0:T(8,128)(2,1)S(1)}, u32[]{:S(2)}, u32[]{:S(2)}) collective-permute-start(bf16[320,2048]{1,0:T(8,128)(2,1)S(1)} %get-tuple-element.46), channel_id=1, source_target_pairs={{0,0},{1,1},{2,32},{3,33},{32,2},{33,3},{34,34},{35,35},{4,4},{5,5... | collective-permute-start | bytes 3932168 | tf_op jit(solution)/shard_map/ppermute | solution.py:273
  23.5 1.5 collective-permute-start.3
  26.2 1.5 collective-permute-start.13
  27.7 1.6 collective-permute-start.4
  29.3 6.1 %collective-permute-done.12 = bf16[128,2048]{1,0:T(8,128)(2,1)S(1)} collective-permute-done((bf16[128,2048]{1,0:T(8,128)(2,1)S(1)}, bf16[128,2048]{1,0:T(8,128)(2,1)S(1)}, u32[]{:S(2)}, u32[]{:S(2)}) %collective-permute-start.12) | collective-permute-done | bytes 524320 | tf_op jit(solution)/shard_map/ppermute | solution.py:253
  36.5 2.7 %collective-permute-start.11 = (bf16[128,2048]{1,0:T(8,128)(2,1)S(1)}, bf16[128,2048]{1,0:T(8,128)(2,1)S(1)}, u32[]{:S(2)}, u32[]{:S(2)}) collective-permute-start(bf16[128,2048]{1,0:T(8,128)(2,1)S(1)} %collective-permute-done.1.args_11_.args_13_), channel_id=1, source_target_pairs={{0,4},{4,0},{1,5},{5,1},{2,6},{6,2},{3,7},{7,3},{8,12},{12,8},{9,1... | collective-permute-start | bytes 1572872 | tf_op jit(solution)/shard_map/ppermute | solution.py:261
  40.8 5.4 %collective-permute-done.5.args_5_.args_7_ = bf16[128,2048]{1,0:T(8,128)(2,1)S(1)} collective-permute-done((bf16[128,2048]{1,0:T(8,128)(2,1)S(1)}, bf16[128,2048]{1,0:T(8,128)(2,1)S(1)}, u32[]{:S(2)}, u32[]{:S(2)}) %collective-permute-start.5) | collective-permute-done | bytes 524320 | tf_op jit(solution)/shard_map/ppermute | solution.py:253
  50.7 1.7 collective-permute-start.7
  52.4 3.4 %collective-permute-done.3.args_2_.args_3_ = bf16[320,2048]{1,0:T(8,128)(2,1)} collective-permute-done((bf16[320,2048]{1,0:T(8,128)(2,1)S(1)}, bf16[320,2048]{1,0:T(8,128)(2,1)}, u32[]{:S(2)}, u32[]{:S(2)}) %collective-permute-start.3) | collective-permute-done | bytes 1310752 | tf_op jit(solution)/shard_map/ppermute | solution.py:273
  58.9 7.0 %collective-permute-done.8.args_8_.args_10_ = bf16[128,2048]{1,0:T(8,128)(2,1)S(1)} collective-permute-done((bf16[128,2048]{1,0:T(8,128)(2,1)S(1)}, bf16[128,2048]{1,0:T(8,128)(2,1)S(1)}, u32[]{:S(2)}, u32[]{:S(2)}) %collective-permute-start.8) | collective-permute-done | bytes 524320 | tf_op jit(solution)/shard_map/ppermute | solution.py:253
  68.6 1.9 %collective-permute-start.10 = (bf16[128,2048]{1,0:T(8,128)(2,1)S(1)}, bf16[128,2048]{1,0:T(8,128)(2,1)}, u32[]{:S(2)}, u32[]{:S(2)}) collective-permute-start(bf16[128,2048]{1,0:T(8,128)(2,1)S(1)} %collective-permute-done.8.args_8_.args_10_), channel_id=1, source_target_pairs={{0,24},{8,0},{16,8},{24,16},{1,25},{9,1},{17,9},{25,17},{2,26},{10... | collective-permute-start | bytes 1572872 | tf_op jit(solution)/shard_map/ppermute | solution.py:253
  71.2 11.3 %collective-permute-done.9.args_9_.args_11_ = bf16[128,2048]{1,0:T(8,128)(2,1)} collective-permute-done((bf16[128,2048]{1,0:T(8,128)(2,1)S(1)}, bf16[128,2048]{1,0:T(8,128)(2,1)}, u32[]{:S(2)}, u32[]{:S(2)}) %collective-permute-start.9) | collective-permute-done | bytes 524320 | tf_op jit(solution)/shard_map/ppermute | solution.py:253
  82.5 7.0 %collective-permute-done.16.args_14_.args_16_ = bf16[384,2048]{1,0:T(8,128)(2,1)S(1)} collective-permute-done((bf16[384,2048]{1,0:T(8,128)(2,1)S(1)}, bf16[384,2048]{1,0:T(8,128)(2,1)S(1)}, u32[]{:S(2)}, u32[]{:S(2)}) %collective-permute-start.16) | collective-permute-done | bytes 1572896 | tf_op jit(solution)/shard_map/ppermute | solution.py:261
  90.6 3.5 %collective-permute-done.22.args_20_.args_22_ = bf16[128,2048]{1,0:T(8,128)(2,1)S(1)} collective-permute-done((bf16[128,2048]{1,0:T(8,128)(2,1)S(1)}, bf16[128,2048]{1,0:T(8,128)(2,1)S(1)}, u32[]{:S(2)}, u32[]{:S(2)}) %collective-permute-start.22) | collective-permute-done | bytes 524320 | tf_op jit(solution)/shard_map/ppermute | solution.py:261
  97.2 7.2 %half.1 = (bf16[16,144,128]{2,1,0:T(8,128)(2,1)}, f32[128,2048]{1,0:T(8,128)}) custom-call(s32[4]{0:T(128)} %pad_add_fusion.args_0_, bf16[320,2048]{1,0:T(8,128)(2,1)} %copy-done.2, bf16[320,2048]{1,0:T(8,128)(2,1)} %collective-permute-done.3.args_2_.args_3_, bf16[128,2048]{1,0:T(8,128)(2,1)} %copy-done.4, bf16[128,2048]{1,0:T(8,128)(2,1)} %copy-done.5, ...), custom_call_target="tpu_custom_call" | custom-call | flops 2147483648 | bytes 12582912 | tf_op jit(solution)/shard_map/half/pallas_call | solution.py:212
  104.4 15.8 %all_to_all.22.args_1_ = bf16[16,144,128]{2,1,0:T(8,128)(2,1)} all-to-all(bf16[16,144,128]{2,1,0:T(8,128)(2,1)} %get-tuple-element.31), channel_id=1, replica_groups=mesh['zh'=4,'c'=2,'x'=4,'zl'=2,'y'=4] {'x','zl','c'}, dimensions={0} | all-to-all | bytes 1179648 | tf_op jit(solution)/shard_map/all_to_all | solution.py:320
  120.2 10.7 %left.1 = (bf16[16,144,128]{2,1,0:T(8,128)(2,1)}, bf16[128,2048]{1,0:T(8,128)(2,1)}, bf16[128,2048]{1,0:T(8,128)(2,1)}, f32[128,2048]{1,0:T(8,128)}) custom-call(s32[4]{0:T(128)} %pad_add_fusion.args_0_, bf16[16,144,128]{2,1,0:T(8,128)(2,1)} %all_to_all.22.args_1_, bf16[320,2048]{1,0:T(8,128)(2,1)} %copy-done.2, ...), custom_call_target="tpu_custom_call" | custom-call | flops 3221225472 | bytes 12582912 | tf_op jit(solution)/shard_map/left/pallas_call | solution.py:212
  130.9 4.0 %all-to-all-start.1 = ((bf16[16,144,128]{2,1,0:T(8,128)(2,1)}), bf16[16,144,128]{2,1,0:T(8,128)(2,1)S(1)}, u32[]{:S(2)}, u32[]{:S(2)}) async-start(bf16[16,144,128]{2,1,0:T(8,128)(2,1)} %get-tuple-element.33), calls=%async_computation.1 | async-start | bytes 1179648 | tf_op jit(solution)/shard_map/all_to_all | solution.py:322
  135.0 10.6 %all-to-all-done.1.args_1_ = bf16[16,144,128]{2,1,0:T(8,128)(2,1)S(1)} async-done(((bf16[16,144,128]{2,1,0:T(8,128)(2,1)}), bf16[16,144,128]{2,1,0:T(8,128)(2,1)S(1)}, u32[]{:S(2)}, u32[]{:S(2)}) %all-to-all-start.1) | async-done | bytes 589856 | tf_op jit(solution)/shard_map/all_to_all | solution.py:322
  145.6 3.9 %collective-permute-start.31 = (bf16[128,2048]{1,0:T(8,128)(2,1)}, bf16[128,2048]{1,0:T(8,128)(2,1)S(1)}, u32[]{:S(2)}, u32[]{:S(2)}) collective-permute-start(bf16[128,2048]{1,0:T(8,128)(2,1)} %get-tuple-element.39), channel_id=1, source_target_pairs={{0,0},{1,1},{32,2},{33,3},{2,32},{3,33},{34,34},{35,35},{4,4},{5,5... | collective-permute-start | bytes 1572872 | tf_op jit(solution)/shard_map/ppermute | solution.py:277
  149.5 4.7 %collective-permute-start.32 = (bf16[128,2048]{1,0:T(8,128)(2,1)}, bf16[128,2048]{1,0:T(8,128)(2,1)S(1)}, u32[]{:S(2)}, u32[]{:S(2)}) collective-permute-start(bf16[128,2048]{1,0:T(8,128)(2,1)} %get-tuple-element.41), channel_id=1, source_target_pairs={{1,0},{0,1},{33,2},{32,3},{3,32},{2,33},{35,34},{34,35},{5,4},{4,5... | collective-permute-start | bytes 1572872 | tf_op jit(solution)/shard_map/ppermute | solution.py:277
  154.2 7.9 %raw.1 = (bf16[128,2048]{1,0:T(8,128)(2,1)}, bf16[128,2048]{1,0:T(8,128)(2,1)}, f32[256,128]{1,0:T(8,128)}) custom-call(s32[4]{0:T(128)} %pad_add_fusion.args_0_, bf16[16,144,128]{2,1,0:T(8,128)(2,1)} %copy-done.21, f32[128,2048]{1,0:T(8,128)} %get-tuple-element.34.args_2_, bf16[128,2048]{1,0:T(8,128)(2,1)} %copy-done.4, bf16[128,2048]{1,0:T(8,128)(2,1)} %copy-done.5, ...), custom_call_target="tpu_custom_call" | custom-call | flops 1073741824 | bytes 12582912 | tf_op jit(solution)/shard_map/raw/pallas_call | solution.py:212
  162.1 2.1 %collective-permute-start.29 = (bf16[128,2048]{1,0:T(8,128)(2,1)}, bf16[128,2048]{1,0:T(8,128)(2,1)}, u32[]{:S(2)}, u32[]{:S(2)}) collective-permute-start(bf16[128,2048]{1,0:T(8,128)(2,1)} %get-tuple-element.35), channel_id=1, source_target_pairs={{0,0},{1,1},{32,2},{33,3},{2,32},{3,33},{34,34},{35,35},{4,4},{5,5... | collective-permute-start | bytes 1572872 | tf_op jit(solution)/shard_map/ppermute | solution.py:277
  164.3 8.8 %all-to-all-start.2 = ((f32[256,1,128]{2,1,0:T(1,128)}), f32[256,1,128]{2,1,0:T(1,128)S(1)}, u32[]{:S(2)}, u32[]{:S(2)}) async-start(f32[256,1,128]{2,1,0:T(1,128)} %bitcast.63), calls=%async_computation.2 | async-start | bytes 262144 | tf_op jit(solution)/shard_map/all_to_all | solution.py:325
  173.3 1.6 fusion.3
  175.8 4.9 %collective-permute-done.30 = bf16[128,2048]{1,0:T(8,128)(2,1)} collective-permute-done((bf16[128,2048]{1,0:T(8,128)(2,1)}, bf16[128,2048]{1,0:T(8,128)(2,1)}, u32[]{:S(2)}, u32[]{:S(2)}) %collective-permute-start.30) | collective-permute-done | bytes 524320 | tf_op jit(solution)/shard_map/ppermute | solution.py:277
  180.7 1.7 maximum_select_fusion
  183.3 2.5 %all-to-all-done.2 = f32[256,1,128]{2,1,0:T(1,128)S(1)} async-done(((f32[256,1,128]{2,1,0:T(1,128)}), f32[256,1,128]{2,1,0:T(1,128)S(1)}, u32[]{:S(2)}, u32[]{:S(2)}) %all-to-all-start.2) | async-done | bytes 131104 | tf_op jit(solution)/shard_map/all_to_all | solution.py:325
  (124 shorter events, 24.3 us)
Async XLA Ops:
  2.0 13.3 %collective-permute-start.1 = (bf16[128,2048]{1,0:T(8,128)(2,1)S(1)}, bf16[128,2048]{1,0:T(8,128)(2,1)S(1)}, u32[]{:S(2)}, u32[]{:S(2)}) collective-permute-start(bf16[128,2048]{1,0:T(8,128)(2,1)S(1)} %pad_maximum_fusion.1), channel_id=1, source_target_pairs={{0,1},{1,0},{2,33},{3,32},{32,3},{33,2},{34,35},{35,34},{4,5},{5,4... | collective-permute-start | bytes 1572872 | tf_op jit(solution)/shard_map/ppermute | solution.py:273
  6.3 13.9 %collective-permute-start = (bf16[128,2048]{1,0:T(8,128)(2,1)S(1)}, bf16[128,2048]{1,0:T(8,128)(2,1)S(1)}, u32[]{:S(2)}, u32[]{:S(2)}) collective-permute-start(bf16[128,2048]{1,0:T(8,128)(2,1)S(1)} %pad_maximum_fusion), channel_id=1, source_target_pairs={{0,0},{1,1},{2,32},{3,33},{32,2},{33,3},{34,34},{35,35},{4,4},{5,5... | collective-permute-start | bytes 1572872 | tf_op jit(solution)/shard_map/ppermute | solution.py:273
  20.5 30.3 %collective-permute-start.2 = (bf16[320,2048]{1,0:T(8,128)(2,1)S(1)}, bf16[320,2048]{1,0:T(8,128)(2,1)S(1)}, u32[]{:S(2)}, u32[]{:S(2)}) collective-permute-start(bf16[320,2048]{1,0:T(8,128)(2,1)S(1)} %get-tuple-element.46), channel_id=1, source_target_pairs={{0,0},{1,1},{2,32},{3,33},{32,2},{33,3},{34,34},{35,35},{4,4},{5,5... | collective-permute-start | bytes 3932168 | tf_op jit(solution)/shard_map/ppermute | solution.py:273
  23.5 32.4 %collective-permute-start.3 = (bf16[320,2048]{1,0:T(8,128)(2,1)S(1)}, bf16[320,2048]{1,0:T(8,128)(2,1)}, u32[]{:S(2)}, u32[]{:S(2)}) collective-permute-start(bf16[320,2048]{1,0:T(8,128)(2,1)S(1)} %get-tuple-element.45), channel_id=1, source_target_pairs={{0,1},{1,0},{2,33},{3,32},{32,3},{33,2},{34,35},{35,34},{4,5},{5,4... | collective-permute-start | bytes 3932168 | tf_op jit(solution)/shard_map/ppermute | solution.py:273
  25.0 10.4 %collective-permute-start.12 = (bf16[128,2048]{1,0:T(8,128)(2,1)S(1)}, bf16[128,2048]{1,0:T(8,128)(2,1)S(1)}, u32[]{:S(2)}, u32[]{:S(2)}) collective-permute-start(bf16[128,2048]{1,0:T(8,128)(2,1)S(1)} %collective-permute-done.1.args_11_.args_13_), channel_id=1, source_target_pairs={{0,8},{8,16},{16,24},{24,0},{1,9},{9,17},{17,25},{25,1},{2,10},{10... | collective-permute-start | bytes 1572872 | tf_op jit(solution)/shard_map/ppermute | solution.py:253
  26.2 10.3 %collective-permute-start.13 = (bf16[128,2048]{1,0:T(8,128)(2,1)S(1)}, bf16[128,2048]{1,0:T(8,128)(2,1)S(1)}, u32[]{:S(2)}, u32[]{:S(2)}) collective-permute-start(bf16[128,2048]{1,0:T(8,128)(2,1)S(1)} %collective-permute-done.1.args_11_.args_13_), channel_id=1, source_target_pairs={{0,24},{8,0},{16,8},{24,16},{1,25},{9,1},{17,9},{25,17},{2,26},{10... | collective-permute-start | bytes 1572872 | tf_op jit(solution)/shard_map/ppermute | solution.py:253
  27.7 13.1 %collective-permute-start.4 = (bf16[128,2048]{1,0:T(8,128)(2,1)S(1)}, bf16[128,2048]{1,0:T(8,128)(2,1)S(1)}, u32[]{:S(2)}, u32[]{:S(2)}) collective-permute-start(bf16[128,2048]{1,0:T(8,128)(2,1)S(1)} %collective-permute-done.args_3_.args_5_), channel_id=1, source_target_pairs={{0,4},{4,0},{1,5},{5,1},{2,6},{6,2},{3,7},{7,3},{8,12},{12,8},{9,1... | collective-permute-start | bytes 1572872 | tf_op jit(solution)/shard_map/ppermute | solution.py:261
  35.4 10.9 %collective-permute-start.5 = (bf16[128,2048]{1,0:T(8,128)(2,1)S(1)}, bf16[128,2048]{1,0:T(8,128)(2,1)S(1)}, u32[]{:S(2)}, u32[]{:S(2)}) collective-permute-start(bf16[128,2048]{1,0:T(8,128)(2,1)S(1)} %collective-permute-done.args_3_.args_5_), channel_id=1, source_target_pairs={{0,8},{8,16},{16,24},{24,0},{1,9},{9,17},{17,25},{25,1},{2,10},{10... | collective-permute-start | bytes 1572872 | tf_op jit(solution)/shard_map/ppermute | solution.py:253
  36.5 12.0 %collective-permute-start.11 = (bf16[128,2048]{1,0:T(8,128)(2,1)S(1)}, bf16[128,2048]{1,0:T(8,128)(2,1)S(1)}, u32[]{:S(2)}, u32[]{:S(2)}) collective-permute-start(bf16[128,2048]{1,0:T(8,128)(2,1)S(1)} %collective-permute-done.1.args_11_.args_13_), channel_id=1, source_target_pairs={{0,4},{4,0},{1,5},{5,1},{2,6},{6,2},{3,7},{7,3},{8,12},{12,8},{9,1... | collective-permute-start | bytes 1572872 | tf_op jit(solution)/shard_map/ppermute | solution.py:261
  40.7 8.5 %collective-permute-start.6 = (bf16[128,2048]{1,0:T(8,128)(2,1)S(1)}, bf16[128,2048]{1,0:T(8,128)(2,1)S(1)}, u32[]{:S(2)}, u32[]{:S(2)}) collective-permute-start(bf16[128,2048]{1,0:T(8,128)(2,1)S(1)} %collective-permute-done.args_3_.args_5_), channel_id=1, source_target_pairs={{0,24},{8,0},{16,8},{24,16},{1,25},{9,1},{17,9},{25,17},{2,26},{10... | collective-permute-start | bytes 1572872 | tf_op jit(solution)/shard_map/ppermute | solution.py:253
  46.2 9.7 %collective-permute-start.14 = (bf16[64,2048]{1,0:T(8,128)(2,1)S(1)}, bf16[64,2048]{1,0:T(8,128)(2,1)S(1)}, u32[]{:S(2)}, u32[]{:S(2)}) collective-permute-start(bf16[64,2048]{1,0:T(8,128)(2,1)S(1)} %slice.36), channel_id=1, source_target_pairs={{0,8},{8,16},{16,24},{24,0},{1,9},{9,17},{17,25},{25,1},{2,10},{10... | collective-permute-start | bytes 786440 | tf_op jit(solution)/shard_map/ppermute | solution.py:253
  48.5 8.5 %collective-permute-start.15 = (bf16[64,2048]{1,0:T(8,128)(2,1)S(1)}, bf16[64,2048]{1,0:T(8,128)(2,1)S(1)}, u32[]{:S(2)}, u32[]{:S(2)}) collective-permute-start(bf16[64,2048]{1,0:T(8,128)(2,1)S(1)} %slice.37), channel_id=1, source_target_pairs={{0,24},{8,0},{16,8},{24,16},{1,25},{9,1},{17,9},{25,17},{2,26},{10... | collective-permute-start | bytes 786440 | tf_op jit(solution)/shard_map/ppermute | solution.py:253
  49.3 16.6 %collective-permute-start.8 = (bf16[128,2048]{1,0:T(8,128)(2,1)S(1)}, bf16[128,2048]{1,0:T(8,128)(2,1)S(1)}, u32[]{:S(2)}, u32[]{:S(2)}) collective-permute-start(bf16[128,2048]{1,0:T(8,128)(2,1)S(1)} %collective-permute-done.4.args_4_.args_6_), channel_id=1, source_target_pairs={{0,24},{8,0},{16,8},{24,16},{1,25},{9,1},{17,9},{25,17},{2,26},{10... | collective-permute-start | bytes 1572872 | tf_op jit(solution)/shard_map/ppermute | solution.py:253
  50.7 15.2 %collective-permute-start.7 = (bf16[128,2048]{1,0:T(8,128)(2,1)S(1)}, bf16[128,2048]{1,0:T(8,128)(2,1)}, u32[]{:S(2)}, u32[]{:S(2)}) collective-permute-start(bf16[128,2048]{1,0:T(8,128)(2,1)S(1)} %collective-permute-done.4.args_4_.args_6_), channel_id=1, source_target_pairs={{0,8},{8,16},{16,24},{24,0},{1,9},{9,17},{17,25},{25,1},{2,10},{10... | collective-permute-start | bytes 1572872 | tf_op jit(solution)/shard_map/ppermute | solution.py:253
  57.1 32.4 %collective-permute-start.16 = (bf16[384,2048]{1,0:T(8,128)(2,1)S(1)}, bf16[384,2048]{1,0:T(8,128)(2,1)S(1)}, u32[]{:S(2)}, u32[]{:S(2)}) collective-permute-start(bf16[384,2048]{1,0:T(8,128)(2,1)S(1)} %constant_dynamic-update-slice_fusion.args_13_.args_15_), channel_id=1, source_target_pairs={{0,4},{4,0},{1,5},{5,1},{2,6},{6,2},{3,7},{7,3},{8,12},{12,8},{9,1... | collective-permute-start | bytes 4718600 | tf_op jit(solution)/shard_map/ppermute | solution.py:261
  58.4 8.1 %collective-permute-start.25 = (bf16[128,2048]{1,0:T(8,128)(2,1)S(1)}, bf16[128,2048]{1,0:T(8,128)(2,1)S(1)}, u32[]{:S(2)}, u32[]{:S(2)}) collective-permute-start(bf16[128,2048]{1,0:T(8,128)(2,1)S(1)} %collective-permute-done.1.args_11_.args_13_), channel_id=1, source_target_pairs={{0,32},{32,0},{1,33},{33,1},{2,34},{34,2},{3,35},{35,3},{4,36},{36... | collective-permute-start | bytes 1572872 | tf_op jit(solution)/shard_map/ppermute | solution.py:261
  58.4 8.3 %collective-permute-start.17 = (bf16[128,2048]{1,0:T(8,128)(2,1)S(1)}, bf16[128,2048]{1,0:T(8,128)(2,1)S(1)}, u32[]{:S(2)}, u32[]{:S(2)}) collective-permute-start(bf16[128,2048]{1,0:T(8,128)(2,1)S(1)} %collective-permute-done.args_3_.args_5_), channel_id=1, source_target_pairs={{0,32},{32,0},{1,33},{33,1},{2,34},{34,2},{3,35},{35,3},{4,36},{36... | collective-permute-start | bytes 1572872 | tf_op jit(solution)/shard_map/ppermute | solution.py:261
  66.4 4.1 %collective-permute-start.26 = (bf16[128,2048]{1,0:T(8,128)(2,1)S(1)}, bf16[128,2048]{1,0:T(8,128)(2,1)S(1)}, u32[]{:S(2)}, u32[]{:S(2)}) collective-permute-start(bf16[128,2048]{1,0:T(8,128)(2,1)S(1)} %collective-permute-done.11.args_12_.args_14_), channel_id=1, source_target_pairs={{0,32},{32,0},{1,33},{33,1},{2,34},{34,2},{3,35},{35,3},{4,36},{36... | collective-permute-start | bytes 1572872 | tf_op jit(solution)/shard_map/ppermute | solution.py:261
  66.7 4.5 %collective-permute-start.20 = (bf16[128,2048]{1,0:T(8,128)(2,1)S(1)}, bf16[128,2048]{1,0:T(8,128)(2,1)S(1)}, u32[]{:S(2)}, u32[]{:S(2)}) collective-permute-start(bf16[128,2048]{1,0:T(8,128)(2,1)S(1)} %collective-permute-done.6.args_6_.args_8_), channel_id=1, source_target_pairs={{0,32},{32,0},{1,33},{33,1},{2,34},{34,2},{3,35},{35,3},{4,36},{36... | collective-permute-start | bytes 1572872 | tf_op jit(solution)/shard_map/ppermute | solution.py:261
  67.8 14.7 %collective-permute-start.9 = (bf16[128,2048]{1,0:T(8,128)(2,1)S(1)}, bf16[128,2048]{1,0:T(8,128)(2,1)}, u32[]{:S(2)}, u32[]{:S(2)}) collective-permute-start(bf16[128,2048]{1,0:T(8,128)(2,1)S(1)} %collective-permute-done.5.args_5_.args_7_), channel_id=1, source_target_pairs={{0,8},{8,16},{16,24},{24,0},{1,9},{9,17},{17,25},{25,1},{2,10},{10... | collective-permute-start | bytes 1572872 | tf_op jit(solution)/shard_map/ppermute | solution.py:253
  68.6 14.0 %collective-permute-start.10 = (bf16[128,2048]{1,0:T(8,128)(2,1)S(1)}, bf16[128,2048]{1,0:T(8,128)(2,1)}, u32[]{:S(2)}, u32[]{:S(2)}) collective-permute-start(bf16[128,2048]{1,0:T(8,128)(2,1)S(1)} %collective-permute-done.8.args_8_.args_10_), channel_id=1, source_target_pairs={{0,24},{8,0},{16,8},{24,16},{1,25},{9,1},{17,9},{25,17},{2,26},{10... | collective-permute-start | bytes 1572872 | tf_op jit(solution)/shard_map/ppermute | solution.py:253
  70.5 26.6 %collective-permute-start.27 = (bf16[384,2048]{1,0:T(8,128)(2,1)S(1)}, bf16[384,2048]{1,0:T(8,128)(2,1)}, u32[]{:S(2)}, u32[]{:S(2)}) collective-permute-start(bf16[384,2048]{1,0:T(8,128)(2,1)S(1)} %constant_dynamic-update-slice_fusion.args_13_.args_15_), channel_id=1, source_target_pairs={{0,32},{32,0},{1,33},{33,1},{2,34},{34,2},{3,35},{35,3},{4,36},{36... | collective-permute-start | bytes 4718600 | tf_op jit(solution)/shard_map/ppermute | solution.py:261
  89.5 7.6 %collective-permute-start.28 = (bf16[384,2048]{1,0:T(8,128)(2,1)S(1)}, bf16[384,2048]{1,0:T(8,128)(2,1)}, u32[]{:S(2)}, u32[]{:S(2)}) collective-permute-start(bf16[384,2048]{1,0:T(8,128)(2,1)S(1)} %collective-permute-done.16.args_14_.args_16_), channel_id=1, source_target_pairs={{0,32},{32,0},{1,33},{33,1},{2,34},{34,2},{3,35},{35,3},{4,36},{36... | collective-permute-start | bytes 4718600 | tf_op jit(solution)/shard_map/ppermute | solution.py:261
  89.5 4.5 %collective-permute-start.22 = (bf16[128,2048]{1,0:T(8,128)(2,1)S(1)}, bf16[128,2048]{1,0:T(8,128)(2,1)S(1)}, u32[]{:S(2)}, u32[]{:S(2)}) collective-permute-start(bf16[128,2048]{1,0:T(8,128)(2,1)S(1)} %collective-permute-done.8.args_8_.args_10_), channel_id=1, source_target_pairs={{0,32},{32,0},{1,33},{33,1},{2,34},{34,2},{3,35},{35,3},{4,36},{36... | collective-permute-start | bytes 1572872 | tf_op jit(solution)/shard_map/ppermute | solution.py:261
  90.0 5.9 %collective-permute-start.21 = (bf16[128,2048]{1,0:T(8,128)(2,1)}, bf16[128,2048]{1,0:T(8,128)(2,1)}, u32[]{:S(2)}, u32[]{:S(2)}) collective-permute-start(bf16[128,2048]{1,0:T(8,128)(2,1)} %collective-permute-done.7.args_7_.args_9_), channel_id=1, source_target_pairs={{0,32},{32,0},{1,33},{33,1},{2,34},{34,2},{3,35},{35,3},{4,36},{36... | collective-permute-start | bytes 1572872 | tf_op jit(solution)/shard_map/ppermute | solution.py:261
  90.1 5.8 %collective-permute-start.23 = (bf16[128,2048]{1,0:T(8,128)(2,1)}, bf16[128,2048]{1,0:T(8,128)(2,1)}, u32[]{:S(2)}, u32[]{:S(2)}) collective-permute-start(bf16[128,2048]{1,0:T(8,128)(2,1)} %collective-permute-done.9.args_9_.args_11_), channel_id=1, source_target_pairs={{0,32},{32,0},{1,33},{33,1},{2,34},{34,2},{3,35},{35,3},{4,36},{36... | collective-permute-start | bytes 1572872 | tf_op jit(solution)/shard_map/ppermute | solution.py:261
  130.9 14.7 %all-to-all-start.1 = ((bf16[16,144,128]{2,1,0:T(8,128)(2,1)}), bf16[16,144,128]{2,1,0:T(8,128)(2,1)S(1)}, u32[]{:S(2)}, u32[]{:S(2)}) async-start(bf16[16,144,128]{2,1,0:T(8,128)(2,1)} %get-tuple-element.33), calls=%async_computation.1 | async-start | bytes 1179648 | tf_op jit(solution)/shard_map/all_to_all | solution.py:322
  145.6 27.5 %collective-permute-start.31 = (bf16[128,2048]{1,0:T(8,128)(2,1)}, bf16[128,2048]{1,0:T(8,128)(2,1)S(1)}, u32[]{:S(2)}, u32[]{:S(2)}) collective-permute-start(bf16[128,2048]{1,0:T(8,128)(2,1)} %get-tuple-element.39), channel_id=1, source_target_pairs={{0,0},{1,1},{32,2},{33,3},{2,32},{3,33},{34,34},{35,35},{4,4},{5,5... | collective-permute-start | bytes 1572872 | tf_op jit(solution)/shard_map/ppermute | solution.py:277
  149.5 23.6 %collective-permute-start.32 = (bf16[128,2048]{1,0:T(8,128)(2,1)}, bf16[128,2048]{1,0:T(8,128)(2,1)S(1)}, u32[]{:S(2)}, u32[]{:S(2)}) collective-permute-start(bf16[128,2048]{1,0:T(8,128)(2,1)} %get-tuple-element.41), channel_id=1, source_target_pairs={{1,0},{0,1},{33,2},{32,3},{3,32},{2,33},{35,34},{34,35},{5,4},{4,5... | collective-permute-start | bytes 1572872 | tf_op jit(solution)/shard_map/ppermute | solution.py:277
  162.1 13.7 %collective-permute-start.29 = (bf16[128,2048]{1,0:T(8,128)(2,1)}, bf16[128,2048]{1,0:T(8,128)(2,1)}, u32[]{:S(2)}, u32[]{:S(2)}) collective-permute-start(bf16[128,2048]{1,0:T(8,128)(2,1)} %get-tuple-element.35), channel_id=1, source_target_pairs={{0,0},{1,1},{32,2},{33,3},{2,32},{3,33},{34,34},{35,35},{4,4},{5,5... | collective-permute-start | bytes 1572872 | tf_op jit(solution)/shard_map/ppermute | solution.py:277
  164.2 16.5 %collective-permute-start.30 = (bf16[128,2048]{1,0:T(8,128)(2,1)}, bf16[128,2048]{1,0:T(8,128)(2,1)}, u32[]{:S(2)}, u32[]{:S(2)}) collective-permute-start(bf16[128,2048]{1,0:T(8,128)(2,1)} %get-tuple-element.36), channel_id=1, source_target_pairs={{1,0},{0,1},{33,2},{32,3},{3,32},{2,33},{35,34},{34,35},{5,4},{4,5... | collective-permute-start | bytes 1572872 | tf_op jit(solution)/shard_map/ppermute | solution.py:277
  164.3 21.5 %all-to-all-start.2 = ((f32[256,1,128]{2,1,0:T(1,128)}), f32[256,1,128]{2,1,0:T(1,128)S(1)}, u32[]{:S(2)}, u32[]{:S(2)}) async-start(f32[256,1,128]{2,1,0:T(1,128)} %bitcast.63), calls=%async_computation.2 | async-start | bytes 262144 | tf_op jit(solution)/shard_map/all_to_all | solution.py:325
  (31 other events, 565.9 us)
